TPU v7x, 32 devices: a whole 2x2x4 slice. The times are simulated.
32 devices in a mesh: ka: 8 (over z, y), ba: 4 (over x, core).
Axes of the slice: x: 2, y: 2, z: 4, core: 2. Of those that a mesh axis runs over, the one named last changes fastest.
Arguments:
- green_irr: bfloat16 [8, 2, 768, 768], P('ka', None, 'ba'), may hold values from -48 to 48
- screened: bfloat16 [128, 768, 768], P('ka', 'ba'), may hold values from -0.75 to 0.75
- kmap: int32 [128, 1], replicated, may hold values from 0 to 7
- rotation: int32 [128, 768], replicated, may hold values from -768 to 767, as said below
Outputs:
- sigma_irr: float32 [8, 2, 768, 768], P('ka', None, 'ba')
Inputs may be any that keep to these rules, and one draw needn't show every extreme that they name: `kmap`: each of the 8 irreducible points is named by one or more k-points. `rotation`: for every k, the sources of the 768 functions are a permutation of them that maps the 6 functions of each atom among themselves (atom n holds functions n * 6 to n * 6 + 5); v >= 0 means source v with sign 1, v < 0 means source -1 - v with sign -1.
All inputs are finite; a program needn't handle non-finite values.
Results may differ from a plain program's by a relative error of at most 0.0065.
Values may be sent and summed in bfloat16 or wider, within the bound.
A program may use at most 64 MiB of HBM per device.

v0:
```python
import math

import jax
import jax.numpy as jnp
from jax import lax
from jax.sharding import PartitionSpec as P

KX = 8
KY = 4
KZ = 4


def decode(rotation):
    source = jnp.where(rotation >= 0, rotation, -1 - rotation)
    signs = jnp.where(rotation >= 0, 1.0, -1.0).astype(jnp.bfloat16)
    return (source, signs)


def phase_tables(count):
    index = jnp.arange(count, dtype=jnp.int32)
    first = index // (KY * KZ)
    second = index // KZ % KY
    third = index % KZ
    turns = first[:, None] * first[None, :] + second[:, None] * second[None, :] * (KX // KY)
    turns = (turns + third[:, None] * third[None, :] * (KX // KZ)) % KX
    angle = turns.astype(jnp.float32) * (2.0 * math.pi / KX)
    return (jnp.cos(angle).astype(jnp.bfloat16), jnp.sin(angle).astype(jnp.bfloat16))


def turn_tables(local_source, local_signs, width):
    places = jnp.arange(width, dtype=jnp.int32)
    same = (local_source[:, :, None] == places[None, None, :]).astype(jnp.bfloat16)
    return same * local_signs[:, :, None]


def turn_forward(block, row_turn, col_turn):
    half = jnp.einsum("kab,kcbd->kcad", row_turn, block, preferred_element_type=jnp.float32).astype(
        jnp.bfloat16
    )
    return jnp.einsum("kcad,ked->kcae", half, col_turn, preferred_element_type=jnp.float32).astype(
        jnp.bfloat16
    )


def turn_back(block, row_turn, col_turn):
    half = jnp.einsum("kab,kcad->kcbd", row_turn, block, preferred_element_type=jnp.float32).astype(
        jnp.bfloat16
    )
    return jnp.einsum("kcbd,kde->kcbe", half, col_turn, preferred_element_type=jnp.float32).astype(
        jnp.bfloat16
    )


def per_device(green_irr, screened, kmap, rotation):
    width_ka = lax.axis_size("ka")
    place_ka = lax.axis_index("ka")
    place_ba = lax.axis_index("ba")
    zone = rotation.shape[0]
    basis = rotation.shape[1]
    rows = green_irr.shape[2]
    cols = basis // width_ka
    wedges = green_irr.shape[0] * width_ka
    row_start = place_ba * rows
    col_start = place_ka * cols
    targets = kmap[:, 0]
    source, signs = decode(rotation)
    cos_t, sin_t = phase_tables(zone)
    counts = jnp.sum(
        (targets[:, None] == jnp.arange(wedges, dtype=jnp.int32)[None, :]).astype(jnp.float32),
        axis=0,
    )
    src_rows = lax.dynamic_slice_in_dim(source, row_start, rows, 1) - row_start
    sgn_rows = lax.dynamic_slice_in_dim(signs, row_start, rows, 1)
    moved = lax.all_to_all(green_irr, "ka", split_axis=3, concat_axis=0, tiled=True)
    src_cols = lax.dynamic_slice_in_dim(source, col_start, cols, 1) - col_start
    sgn_cols = lax.dynamic_slice_in_dim(signs, col_start, cols, 1)
    row_turn = turn_tables(src_rows, sgn_rows, rows)
    col_turn = turn_tables(src_cols, sgn_cols, cols)
    pick = (targets[:, None] == jnp.arange(wedges, dtype=jnp.int32)[None, :]).astype(jnp.bfloat16)
    selected = jnp.einsum("kn,ncab->kcab", pick, moved, preferred_element_type=jnp.float32).astype(
        jnp.bfloat16
    )
    green_k = turn_forward(selected, row_turn, col_turn)
    flat = green_k.reshape(zone, 2, rows * cols)
    green_r = (
        (
            jnp.dot(cos_t, flat[:, 0], preferred_element_type=jnp.float32)
            - jnp.dot(sin_t, flat[:, 1], preferred_element_type=jnp.float32)
        )
        * (1.0 / zone)
    ).astype(jnp.bfloat16)
    at_lattice = lax.all_to_all(
        green_r.reshape(zone, rows, cols), "ka", split_axis=0, concat_axis=2, tiled=True
    )
    product = (-(at_lattice.astype(jnp.float32) * screened.astype(jnp.float32))).astype(
        jnp.bfloat16
    )
    sigma_r = lax.all_to_all(product, "ka", split_axis=2, concat_axis=0, tiled=True).reshape(
        zone, rows * cols
    )
    real_k = jnp.dot(cos_t, sigma_r, preferred_element_type=jnp.float32).astype(jnp.bfloat16)
    imag_k = (-jnp.dot(sin_t, sigma_r, preferred_element_type=jnp.float32)).astype(jnp.bfloat16)
    sigma_k = jnp.stack([real_k, imag_k], axis=1).reshape(zone, 2, rows, cols)
    turned = turn_back(sigma_k, row_turn, col_turn)
    hit = (targets[None, :] == jnp.arange(wedges, dtype=jnp.int32)[:, None]).astype(jnp.bfloat16)
    folded = jnp.einsum("ik,kcab->icab", hit, turned, preferred_element_type=jnp.float32)
    folded = folded / counts[:, None, None, None]
    return lax.all_to_all(
        folded.astype(jnp.bfloat16), "ka", split_axis=0, concat_axis=3, tiled=True
    ).astype(folded.dtype)


def solution(mesh):
    placed = (P("ka", None, "ba", None), P("ka", "ba", None), P(), P())
    return jax.shard_map(
        per_device, mesh=mesh, in_specs=placed, out_specs=P("ka", None, "ba", None), check_vma=False
    )
```

profile of v0, /device:TPU:0, one launch (start us, length us, event | category | flops | bytes accessed | tf_op | source)
XLA Modules:
  0.0 573.2 jit_solution(10365865643789767125)
XLA Ops:
  0.0 3.0 copy.62
  3.0 7.3 %all-to-all-start = ((bf16[1,2,192,768]{2,1,0,3:T(2,128)(2,1)}), bf16[1,2,192,768]{2,1,0,3:T(2,128)(2,1)S(1)}, u32[]{:S(2)}, u32[]{:S(2)}) async-start(bf16[1,2,192,768]{2,1,0,3:T(2,128)(2,1)} %copy.62), calls=%async_computation | async-start | bytes 1572864 | tf_op jit(solution)/shard_map/all_to_all | solution.py:74
  10.3 1.0 fusion.68
  11.3 0.1 constant_dynamic-slice_fusion
  11.4 1.0 subtract_select_fusion
  12.5 0.1 dynamic-slice_subtract_fusion.1
  12.6 0.1 constant_dynamic-slice_fusion.1
  12.7 0.1 dynamic-slice_subtract_fusion
  12.8 17.7 %all-to-all-done = bf16[1,2,192,768]{2,1,0,3:T(2,128)(2,1)S(1)} async-done(((bf16[1,2,192,768]{2,1,0,3:T(2,128)(2,1)}), bf16[1,2,192,768]{2,1,0,3:T(2,128)(2,1)S(1)}, u32[]{:S(2)}, u32[]{:S(2)}) %all-to-all-start) | async-done | bytes 589856 | tf_op jit(solution)/shard_map/all_to_all | solution.py:74
  30.4 1.4 copy.88
  31.9 6.7 %convolution_convert_fusion.1 = bf16[128,2,192,96]{0,3,2,1:T(8,128)(2,1)} fusion(bf16[1,2,192,8,96]{4,3,2,1,0:T(8,128)(2,1)S(1)} %copy.88, s32[128]{0:T(128)} %bitcast.115), kind=kOutput, calls=%fused_computation.34 | convolution fusion | flops 80217088 | bytes 10027520 | tf_op jit(solution)/shard_map/kn,ncab->kcab/dot_general | solution.py:80
  38.6 17.8 %copy.64 = bf16[128,2,192,96]{2,3,1,0:T(8,128)(2,1)} copy(bf16[128,2,192,96]{0,3,2,1:T(8,128)(2,1)} %convolution_convert_fusion.1) | data formatting | bytes 18874368 | tf_op jit(solution)/shard_map/convert_element_type | solution.py:80
  56.4 18.3 %fusion.41 = bf16[128,2,192,96]{3,2,1,0:T(8,128)(2,1)} fusion(bf16[128,2,192,96]{2,3,1,0:T(8,128)(2,1)} %copy.64, s32[128,192]{1,0:T(8,128)S(1)} %dynamic-slice_subtract_fusion, bf16[128,192]{1,0:T(8,128)(2,1)S(1)} %constant_dynamic-slice_fusion.1, s32[128,96]{1,0:T(8,128)S(1)} %dynamic-slice_subtract_fusion.1, ...), kind=kOutput, calls=%fused_computation.27 | convolution fusion | flops 2739142656 | bytes 19095552 | tf_op jit(solution)/shard_map/kcad,ked->kcae/dot_general | solution.py:40
  74.7 15.8 %copy.66 = bf16[128,2,192,96]{0,3,2,1:T(8,128)(2,1)} copy(bf16[128,2,192,96]{3,2,1,0:T(8,128)(2,1)} %fusion.41) | data formatting | bytes 18874368 | tf_op jit(solution)/shard_map/convert_element_type | solution.py:40
  90.5 0.0 copy-start.1
  90.5 4.2 fusion.55
  94.7 0.9 copy-done.1
  95.6 3.5 fusion.2
  99.1 6.7 %copy.69 = bf16[128,18432]{0,1:T(8,128)(2,1)} copy(bf16[128,18432]{1,0:T(8,128)(2,1)} %fusion.2) | data formatting | bytes 9437184 | tf_op jit(solution)/shard_map/convert_element_type | solution.py:91
  105.9 8.4 %copy.70 = bf16[128,192,96]{2,1,0:T(8,128)(2,1)} copy(bf16[128,192,96]{0,2,1:T(8,128)(2,1)} %bitcast.111) | data formatting | bytes 9437184 | tf_op jit(solution)/shard_map/reshape | solution.py:93
  114.3 142.0 %all_to_all.51 = bf16[128,192,96]{2,1,0:T(8,128)(2,1)S(1)} all-to-all(bf16[128,192,96]{2,1,0:T(8,128)(2,1)} %copy.70), channel_id=1, replica_groups=mesh['ka'=8,'ba'=4] {'ka'}, dimensions={0} | all-to-all | bytes 9437184 | tf_op jit(solution)/shard_map/all_to_all | solution.py:92
  256.3 6.1 %convert_bitcast_fusion = f32[16,192,8,96]{3,1,0,2:T(8,128)} fusion(bf16[8,16,192,96]{3,2,1,0:T(8,128)(2,1)S(1)} %bitcast.109), kind=kLoop, calls=%fused_computation.14 | loop fusion | flops 2359296 | bytes 14155776 | tf_op jit(solution)/shard_map/convert_element_type | solution.py:95
  262.5 18.9 %copy.71 = f32[16,192,8,96]{3,2,1,0:T(8,128)} copy(f32[16,192,8,96]{3,1,0,2:T(8,128)} %convert_bitcast_fusion) | data formatting | bytes 18874368 | tf_op jit(solution)/shard_map/convert_element_type | solution.py:95
  281.4 13.6 %reshape.132 = f32[16,192,768]{2,1,0:T(8,128)} reshape(f32[16,192,8,96]{3,2,1,0:T(8,128)} %copy.71) | data formatting | bytes 18874368 | tf_op jit(solution)/shard_map/convert_element_type | solution.py:95
  295.0 8.5 %negate_convert_fusion = bf16[16,192,768]{2,1,0:T(8,128)(2,1)} fusion(f32[16,192,768]{2,1,0:T(8,128)} %reshape.132, bf16[16,192,768]{2,1,0:T(8,128)(2,1)} %param.5), kind=kLoop, calls=%fused_computation.25 | loop fusion | flops 9437184 | bytes 18874368 | tf_op jit(solution)/shard_map/convert_element_type | solution.py:95
  303.4 0.0 copy-start.2
  303.4 9.2 %copy.72 = bf16[16,192,768]{1,0,2:T(8,128)(2,1)} copy(bf16[16,192,768]{2,1,0:T(8,128)(2,1)} %negate_convert_fusion) | data formatting | bytes 9437184 | tf_op jit(solution)/shard_map/convert_element_type | solution.py:95
  312.6 4.8 all-to-all-start.2
  317.4 0.0 copy-done.2
  317.4 0.1 convert_reduce_fusion
  317.5 137.1 %all-to-all-done.2 = bf16[16,192,768]{1,0,2:T(8,128)(2,1)} async-done(((bf16[16,192,768]{1,0,2:T(8,128)(2,1)}), bf16[16,192,768]{1,0,2:T(8,128)(2,1)}, u32[]{:S(2)}, u32[]{:S(2)}) %all-to-all-start.2) | async-done | bytes 4718624 | tf_op jit(solution)/shard_map/all_to_all | solution.py:98
  454.6 10.4 %copy.73 = bf16[16,192,8,96]{3,1,0,2:T(8,128)(2,1)} copy(bf16[16,192,8,96]{1,0,3,2:T(8,128)(2,1)} %bitcast.19) | data formatting | bytes 9437184 | tf_op jit(solution)/shard_map/all_to_all | solution.py:98
  465.0 11.7 %reshape.131 = bf16[128,18432]{1,0:T(8,128)(2,1)} reshape(bf16[8,16,192,96]{3,2,1,0:T(8,128)(2,1)} %bitcast.110) | data formatting | bytes 9437184 | tf_op jit(solution)/shard_map/reshape | solution.py:98
  476.7 0.0 copy-start
  476.7 6.3 %convolution_convert_fusion = bf16[128,18432]{1,0:T(8,128)(2,1)} fusion(bf16[128,18432]{1,0:T(8,128)(2,1)} %reshape.131, s32[128]{0:T(128)S(1)} %get-tuple-element.5, s32[128]{0:T(128)S(1)} %get-tuple-element.6, s32[128]{0:T(128)S(1)} %and_select_fusion.3), kind=kOutput, calls=%fused_computation.7 | convolution fusion | flops 606683136 | bytes 9438720 | tf_op jit(solution)/shard_map/dot_general | solution.py:101
  483.0 0.0 copy-done
  483.1 3.9 fusion.3
  487.0 6.7 %copy.74 = bf16[128,18432]{0,1:T(8,128)(2,1)} copy(bf16[128,18432]{1,0:T(8,128)(2,1)} %convolution_convert_fusion) | data formatting | bytes 9437184 | tf_op jit(solution)/shard_map/convert_element_type | solution.py:101
  493.7 9.5 %copy.76 = bf16[128,1,192,96]{2,3,1,0:T(8,128)(2,1)} copy(bf16[128,1,192,96]{0,3,2,1:T(8,128)(2,1)} %bitcast.112) | data formatting | bytes 9437184 | tf_op jit(solution)/shard_map/stack | solution.py:103
  503.2 6.7 %copy.75 = bf16[128,18432]{0,1:T(8,128)(2,1)} copy(bf16[128,18432]{1,0:T(8,128)(2,1)} %fusion.3) | data formatting | bytes 9437184 | tf_op jit(solution)/shard_map/convert_element_type | solution.py:102
  509.8 9.5 %copy.77 = bf16[128,1,192,96]{2,3,1,0:T(8,128)(2,1)} copy(bf16[128,1,192,96]{0,3,2,1:T(8,128)(2,1)} %bitcast.113) | data formatting | bytes 9437184 | tf_op jit(solution)/shard_map/stack | solution.py:103
  519.4 10.7 %fusion.134 = bf16[128,2,192,96]{2,3,1,0:T(8,128)(2,1)S(1)} fusion(s32[128,192]{1,0:T(8,128)S(1)} %dynamic-slice_subtract_fusion, bf16[128,1,192,96]{2,3,1,0:T(8,128)(2,1)} %copy.77, bf16[128,1,192,96]{2,3,1,0:T(8,128)(2,1)} %copy.76, bf16[128,192]{1,0:T(8,128)(2,1)S(1)} %constant_dynamic-slice_fusion.1), kind=kOutput, calls=%fused_computation.16.clone.clone.clone.2 | convolution fusion | flops 1830813696 | bytes 19021824 | tf_op jit(solution)/shard_map/kab,kcad->kcbd/dot_general | solution.py:46
  530.1 9.4 %fusion.34 = bf16[128,2,192,96]{3,2,1,0:T(8,128)(2,1)S(1)} fusion(s32[128,96]{1,0:T(8,128)S(1)} %dynamic-slice_subtract_fusion.1, bf16[128,96]{1,0:T(8,128)(2,1)S(1)} %constant_dynamic-slice_fusion, bf16[128,2,192,96]{2,3,1,0:T(8,128)(2,1)S(1)} %fusion.134), kind=kOutput, calls=%fused_computation.26 | convolution fusion | flops 913047552 | bytes 18948096 | tf_op jit(solution)/shard_map/kcbd,kde->kcbe/dot_general | solution.py:49
  539.5 6.7 %divide_convert_fusion = bf16[8,2,192,96]{3,0,2,1:T(8,128)(2,1)S(1)} fusion(bf16[128,2,192,96]{3,2,1,0:T(8,128)(2,1)S(1)} %fusion.34, f32[8]{0:T(128)S(1)} %convert_reduce_fusion, s32[128]{0:T(128)S(1)} %bitcast.117), kind=kOutput, calls=%fused_computation.42 | convolution fusion | flops 76088320 | bytes 10027552 | tf_op jit(solution)/shard_map/ik,kcab->icab/dot_general | solution.py:106
  546.3 0.1 copy.80
  546.4 23.7 %all_to_all.52 = bf16[8,2,192,96]{3,2,1,0:T(8,128)(2,1)S(1)} all-to-all(bf16[8,2,192,96]{3,2,1,0:T(8,128)(2,1)S(1)} %copy.80), channel_id=1, replica_groups=mesh['ka'=8,'ba'=4] {'ka'}, dimensions={0} | all-to-all | bytes 1179648 | tf_op jit(solution)/shard_map/all_to_all | solution.py:108
  570.1 0.2 convert_bitcast_fusion.1
  570.3 0.9 copy.81
  571.2 1.5 reshape.133
  (2 shorter events, 0.0 us)
Async XLA Ops:
  3.0 27.5 %all-to-all-start = ((bf16[1,2,192,768]{2,1,0,3:T(2,128)(2,1)}), bf16[1,2,192,768]{2,1,0,3:T(2,128)(2,1)S(1)}, u32[]{:S(2)}, u32[]{:S(2)}) async-start(bf16[1,2,192,768]{2,1,0,3:T(2,128)(2,1)} %copy.62), calls=%async_computation | async-start | bytes 1572864 | tf_op jit(solution)/shard_map/all_to_all | solution.py:74
  90.5 5.1 copy-start.1
  303.4 13.9 %copy-start.2 = (s32[128,1]{0,1:T(1,128)S(1)}, s32[128,1]{0,1:T(1,128)}, u32[]{:S(2)}) copy-start(s32[128,1]{0,1:T(1,128)} %param.6) | copy-start | bytes 1540
  312.6 142.0 %all-to-all-start.2 = ((bf16[16,192,768]{1,0,2:T(8,128)(2,1)}), bf16[16,192,768]{1,0,2:T(8,128)(2,1)}, u32[]{:S(2)}, u32[]{:S(2)}) async-start(bf16[16,192,768]{1,0,2:T(8,128)(2,1)} %copy.72), calls=%async_computation.2 | async-start | bytes 12582912 | tf_op jit(solution)/shard_map/all_to_all | solution.py:98
  476.7 6.3 %copy-start = (bf16[128,18432]{1,0:T(8,128)(2,1)S(1)}, bf16[128,18432]{1,0:T(8,128)(2,1)}, u32[]{:S(2)}) copy-start(bf16[128,18432]{1,0:T(8,128)(2,1)} %reshape.131) | copy-start | bytes 14155780
where the time goes:
time: 584 us; the launch traced here: 573 us
  blocking collectives  166 us (28%)
  waiting for transfers between devices  155 us (27%)
  local copies, waits for them, and re-layouts  153 us (26%)
  matrix products  69.9 us (12%)
  other arithmetic  17.2 us (3%)
  starting transfers between devices  12 us (2%)
    all_to_all x1, blocking collectives, per_device(): lax.all_to_all(green_r.reshape(zone, rows, cols), 'ka', split_axis=0, con...  142 us
    all_to_all x1, waiting for transfers between devices, per_device(): lax.all_to_all(product, 'ka', split_axis=2, concat_axis=0, tiled=True)  137 us
    convert_element_type x2, local copies, waits for them, and re-layouts, per_device(): at_lattice.astype(jnp.float32) * screened.astype(jnp.float32)  32.5 us
    all_to_all x1, blocking collectives, per_device(): lax.all_to_all(folded.astype(jnp.bfloat16), 'ka', split_axis=0, concat_ax...  23.7 us
    another operation x2, local copies, waits for them, and re-layouts, per_device(): sigma_k = jnp.stack([real_k, imag_k], axis=1).reshape(zone, 2, rows, cols)  19 us
    dot_general x1, matrix products, turn_forward(): jnp.einsum('kcad,ked->kcae', half, col_turn, preferred_element_type=jnp.f...  18.3 us
    convert_element_type x1, local copies, waits for them, and re-layouts, per_device(): jnp.einsum('kn,ncab->kcab', pick, moved, preferred_element_type=jnp.float32)  17.8 us
    all_to_all x1, waiting for transfers between devices, per_device(): lax.all_to_all(green_irr, 'ka', split_axis=3, concat_axis=0, tiled=True)  17.7 us
  transfers between devices with their start and end apart: 2, of which 2 were waited for; matrix products, arithmetic and copies ran while one was open for 0% of the time, Pallas kernels for 0%

commit v1 on v0

--- a/solution.py
+++ b/solution.py
@@ -3,6 +3,8 @@
 import jax
 import jax.numpy as jnp
 from jax import lax
+from jax.experimental import pallas as pl
+from jax.experimental.pallas import tpu as pltpu
 from jax.sharding import PartitionSpec as P
 
 KX = 8
@@ -51,7 +53,7 @@
     )
 
 
-def per_device(green_irr, screened, kmap, rotation):
+def per_device_columns(green_irr, screened, kmap, rotation):
     width_ka = lax.axis_size("ka")
     place_ka = lax.axis_index("ka")
     place_ba = lax.axis_index("ba")
@@ -110,6 +112,214 @@
     ).astype(folded.dtype)
 
 
+ORB = 6
+
+
+def column_order(basis):
+    atoms = basis // ORB
+    place = jnp.arange(basis, dtype=jnp.int32)
+    moved = (place % ORB) * atoms + place // ORB
+    return (moved[:, None] == place[None, :]).astype(jnp.bfloat16)
+
+
+def prepare_kernel(swap_ref, order_ref, w_ref, out_ref):
+    count, rows, basis = w_ref.shape
+    block = w_ref[...].reshape(count * rows, basis)
+    turned = jnp.dot(swap_ref[...], block, preferred_element_type=jnp.float32).astype(jnp.bfloat16)
+    out = jnp.dot(turned, order_ref[...], preferred_element_type=jnp.float32).astype(jnp.bfloat16)
+    out_ref[...] = out.reshape(rows, count, basis)
+
+
+def prepare(screened, order, step=16):
+    count, rows, basis = screened.shape
+    place = jnp.arange(count * step, dtype=jnp.int32)
+    origin = (place % count) * step + place // count
+    swap = (origin[:, None] == place[None, :]).astype(jnp.bfloat16)
+    return pl.pallas_call(
+        prepare_kernel,
+        grid=(rows // step,),
+        in_specs=[
+            pl.BlockSpec((count * step, count * step), lambda i: (0, 0)),
+            pl.BlockSpec((basis, basis), lambda i: (0, 0)),
+            pl.BlockSpec((count, step, basis), lambda i: (0, i, 0)),
+        ],
+        out_specs=pl.BlockSpec((step, count, basis), lambda i: (i, 0, 0)),
+        out_shape=jax.ShapeDtypeStruct((rows, count, basis), jnp.bfloat16),
+        compiler_params=pltpu.CompilerParams(vmem_limit_bytes=24 << 20),
+        cost_estimate=pl.CostEstimate(
+            flops=4800000000, bytes_accessed=4 * count * rows * basis, transcendentals=0
+        ),
+    )(swap, order, screened)
+
+
+def turn_columns(coef_ref, src, dst, zone, atoms, back):
+    def chunk(step, carry):
+        at = pl.ds(pl.multiple_of(step * 16, 16), 16)
+        coef = [[coef_ref[o, p, at, :] for p in range(ORB)] for o in range(ORB)]
+        for oa in range(ORB):
+            for c in range(2):
+                given = [src(oa, c, p, step) for p in range(ORB)]
+                for o in range(ORB):
+                    total = None
+                    for p in range(ORB):
+                        term = (coef[p][o] if back else coef[o][p]) * given[p]
+                        total = term if total is None else total + term
+                    dst(oa, c, o, step, total)
+        return carry
+
+    lax.fori_loop(0, zone // 16, chunk, 0)
+
+
+def unfold_kernel(select_ref, green_ref, coef_ref, phase_ref, out_ref, half, full):
+    zone = phase_ref.shape[0]
+    basis = out_ref.shape[2]
+    atoms = basis // ORB
+    half[...] = jnp.dot(select_ref[0], green_ref[0], preferred_element_type=jnp.float32).astype(
+        jnp.bfloat16
+    )
+
+    def read(oa, c, p, step):
+        at = pl.ds(pl.multiple_of(oa * zone + step * 16, 16), 16)
+        return half[at, c * basis + p * atoms : c * basis + (p + 1) * atoms]
+
+    def write(oa, c, o, step, value):
+        at = pl.ds(pl.multiple_of(c * zone + step * 16, 16), 16)
+        full[oa, at, o * atoms : (o + 1) * atoms] = value
+
+    turn_columns(coef_ref, read, write, zone, atoms, False)
+    for oa in range(ORB):
+        sums = jnp.dot(phase_ref[...], full[oa], preferred_element_type=jnp.float32)
+        out_ref[oa] = (sums * (1.0 / zone)).astype(jnp.bfloat16)
+
+
+def fold_kernel(select_ref, counts_ref, green_ref, w_ref, coef_ref, phase_ref, out_ref, full, half):
+    zone = phase_ref.shape[1]
+    basis = green_ref.shape[2]
+    atoms = basis // ORB
+    for oa in range(ORB):
+        w = w_ref[:, oa].reshape(zone, basis)
+        sigma = (-(green_ref[oa].astype(jnp.float32) * w.astype(jnp.float32))).astype(jnp.bfloat16)
+        full[oa] = jnp.dot(phase_ref[...], sigma, preferred_element_type=jnp.float32).astype(
+            jnp.bfloat16
+        )
+
+    def read(oa, c, p, step):
+        at = pl.ds(pl.multiple_of(c * zone + step * 16, 16), 16)
+        return full[oa, at, p * atoms : (p + 1) * atoms]
+
+    def write(oa, c, o, step, value):
+        at = pl.ds(pl.multiple_of(oa * zone + step * 16, 16), 16)
+        half[at, c * basis + o * atoms : c * basis + (o + 1) * atoms] = value
+
+    turn_columns(coef_ref, read, write, zone, atoms, True)
+    sums = jnp.dot(select_ref[0], half[...], preferred_element_type=jnp.float32)
+    out_ref[0] = (sums / counts_ref[...]).astype(jnp.bfloat16)
+
+
+def per_device_rows(green_irr, screened, kmap, rotation):
+    width = lax.axis_size("ka")
+    zone, basis = rotation.shape
+    atoms = basis // ORB
+    own, _, rows, _ = green_irr.shape
+    wedges = own * width
+    part = rows // width
+    sites = part // ORB
+    near = screened.shape[0]
+    targets = kmap[:, 0]
+    order = column_order(basis)
+
+    sent = prepare(screened, order).reshape(width, part, near, basis)
+    w = lax.all_to_all(sent, "ka", split_axis=0, concat_axis=0, tiled=True)
+
+    green = jnp.dot(
+        green_irr.reshape(own * 2 * rows, basis), order, preferred_element_type=jnp.float32
+    ).astype(jnp.bfloat16)
+    green = green.reshape(own, 2, width, part, basis).transpose(2, 0, 1, 3, 4)
+    green = lax.all_to_all(green, "ka", split_axis=0, concat_axis=0, tiled=True)
+    green = green.reshape(wedges, 2, sites, ORB, basis).transpose(2, 0, 3, 1, 4)
+    green = green.reshape(sites, wedges * ORB, 2 * basis)
+
+    cos_t, sin_t = phase_tables(zone)
+    source, signs = decode(rotation)
+    orbital = jnp.arange(ORB, dtype=jnp.int32)
+    place = source - (jnp.arange(basis, dtype=jnp.int32) // ORB * ORB)[None, :]
+    place = place.reshape(zone, atoms, ORB).transpose(2, 0, 1)
+    sign = signs.reshape(zone, atoms, ORB).transpose(2, 0, 1)
+    coef = (place[:, None] == orbital[None, :, None, None]).astype(jnp.bfloat16) * sign[:, None]
+
+    first = lax.axis_index("ba") * rows // ORB + lax.axis_index("ka") * sites
+    row_place = lax.dynamic_slice_in_dim(place, first, sites, 2).transpose(2, 0, 1)
+    row_sign = lax.dynamic_slice_in_dim(sign, first, sites, 2).transpose(2, 0, 1)
+    code = targets[None, None, :] * ORB + row_place
+    hit = jnp.arange(wedges * ORB, dtype=jnp.int32)
+    code = code.reshape(sites, ORB * zone)
+    row_sign = row_sign.reshape(sites, ORB * zone)
+    select = (code[:, :, None] == hit[None, None, :]).astype(jnp.bfloat16) * row_sign[:, :, None]
+    back = (code[:, None, :] == hit[None, :, None]).astype(jnp.bfloat16) * row_sign[:, None, :]
+    counts = jnp.sum(
+        (targets[None, :] == (hit // ORB)[:, None]).astype(jnp.float32), axis=1, keepdims=True
+    )
+
+    whole = lambda shape: pl.BlockSpec(shape, lambda i: (0,) * len(shape))
+    params = pltpu.CompilerParams(vmem_limit_bytes=40 << 20)
+    cost = pl.CostEstimate(flops=12000000000, bytes_accessed=12 << 20, transcendentals=0)
+    green_r = pl.pallas_call(
+        unfold_kernel,
+        grid=(sites,),
+        in_specs=[
+            pl.BlockSpec((1, ORB * zone, wedges * ORB), lambda i: (i, 0, 0)),
+            pl.BlockSpec((1, wedges * ORB, 2 * basis), lambda i: (i, 0, 0)),
+            whole(coef.shape),
+            whole((zone, 2 * zone)),
+        ],
+        out_specs=pl.BlockSpec((ORB, zone, basis), lambda i: (i, 0, 0)),
+        out_shape=jax.ShapeDtypeStruct((part, zone, basis), jnp.bfloat16),
+        scratch_shapes=[
+            pltpu.VMEM((ORB * zone, 2 * basis), jnp.bfloat16),
+            pltpu.VMEM((ORB, 2 * zone, basis), jnp.bfloat16),
+        ],
+        compiler_params=params,
+        cost_estimate=cost,
+    )(select, green, coef, jnp.concatenate([cos_t, -sin_t], axis=1))
+    folded = pl.pallas_call(
+        fold_kernel,
+        grid=(sites,),
+        in_specs=[
+            pl.BlockSpec((1, wedges * ORB, ORB * zone), lambda i: (i, 0, 0)),
+            whole((wedges * ORB, 1)),
+            pl.BlockSpec((ORB, zone, basis), lambda i: (i, 0, 0)),
+            pl.BlockSpec((width, ORB, near, basis), lambda i: (0, i, 0, 0)),
+            whole(coef.shape),
+            whole((2 * zone, zone)),
+        ],
+        out_specs=pl.BlockSpec((1, wedges * ORB, 2 * basis), lambda i: (i, 0, 0)),
+        out_shape=jax.ShapeDtypeStruct((sites, wedges * ORB, 2 * basis), jnp.bfloat16),
+        scratch_shapes=[
+            pltpu.VMEM((ORB, 2 * zone, basis), jnp.bfloat16),
+            pltpu.VMEM((ORB * zone, 2 * basis), jnp.bfloat16),
+        ],
+        compiler_params=params,
+        cost_estimate=cost,
+    )(back, counts, green_r, w, coef, jnp.concatenate([cos_t, -sin_t], axis=0))
+
+    folded = folded.reshape(sites, wedges, ORB, 2, basis).transpose(1, 3, 0, 2, 4)
+    folded = folded.reshape(width, own, 2, part, basis)
+    folded = lax.all_to_all(folded, "ka", split_axis=0, concat_axis=0, tiled=True)
+    folded = folded.transpose(1, 2, 0, 3, 4).reshape(own * 2 * rows, basis)
+    out = lax.dot_general(
+        folded, order, (((1,), (1,)), ((), ())), preferred_element_type=jnp.float32
+    )
+    return out.reshape(own, 2, rows, basis)
+
+
+def per_device(green_irr, screened, kmap, rotation):
+    rows = green_irr.shape[2]
+    width = lax.axis_size("ka")
+    if rows % (width * ORB) == 0 and screened.shape[0] % 16 == 0:
+        return per_device_rows(green_irr, screened, kmap, rotation)
+    return per_device_columns(green_irr, screened, kmap, rotation)
+
+
 def solution(mesh):
     placed = (P("ka", None, "ba", None), P("ka", "ba", None), P(), P())
     return jax.shard_map(

time: 584 us -> 175 us (0.30); the launches traced: 573 us -> 174 us
  blocking collectives: 166 us -> 20.1 us
  local copies, waits for them, and re-layouts: 153 us -> 18.5 us
  waiting for transfers between devices: 155 us -> 79 us
  matrix products: 69.9 us -> 2.6 us
  Pallas kernels: 0 us -> 37 us
  other arithmetic: 17.2 us -> 4.51 us
    all_to_all x2 -> x1, blocking collectives: 166 us -> 20.1 us  [per_device_rows(): lax.all_to_all(folded, 'ka', split_axis=0, concat_axis=0, tiled=True)]
    convert_element_type x11 -> x1, local copies, waits for them, and re-layouts: 97.9 us -> 0.16 us  [decode(): signs = jnp.where(rotation >= 0, 1.0, -1.0).astype(jnp.bfloat16)]
    all_to_all x2, waiting for transfers between devices: 155 us -> 79 us  [the longest x1 76.6 us: per_device_rows(): w = lax.all_to_all(sent, 'ka', split_axis=0, concat_axis=0, tiled=True)]
    dot_general x9 -> x2, matrix products: 69.9 us -> 2.6 us  [the longest x1 1.78 us: per_device_rows(): lax.dot_general(folded, order, (((1,), (1,)), ((), ())), preferred_elemen...]
    pallas_call x0 -> x3, Pallas kernels: none -> 37 us  [the longest x1 15.1 us: per_device_rows(): pl.pallas_call(fold_kernel, grid=(sites,), in_specs=[pl.BlockSpec((1, wed...]
    another operation x2 -> x0, local copies, waits for them, and re-layouts: 19 us -> none  [per_device(): sigma_k = jnp.stack([real_k, imag_k], axis=1).reshape(zone, 2, rows, cols)]
    reshape x2 -> x7, local copies, waits for them, and re-layouts: 20.1 us -> 3.38 us  [the longest x1 2.11 us: per_device_rows(): green = green.reshape(sites, wedges * ORB, 2 * basis)]
    convert_element_type x3, other arithmetic: 14.8 us -> 0.71 us  [the longest x1 0.35 us: phase_tables(): jnp.cos(angle).astype(jnp.bfloat16)]
  transfers between devices with their start and end apart: 2 -> 2, of which waited for: 2 -> 2; matrix products, arithmetic and copies ran while one was open for 0% -> 6% of each run, Pallas kernels for 0% -> 13%
where the time goes in v1:
time: 175 us; the launch traced here: 174 us
  waiting for transfers between devices  79 us (45%)
  Pallas kernels  37 us (21%)
  blocking collectives  20.1 us (11%)
  local copies, waits for them, and re-layouts  18.5 us (11%)
  starting transfers between devices  12 us (7%)
  other arithmetic  4.51 us (3%)
  matrix products  2.6 us (1%)
    all_to_all x1, waiting for transfers between devices, per_device_rows(): w = lax.all_to_all(sent, 'ka', split_axis=0, concat_axis=0, tiled=True)  76.6 us
    all_to_all x1, blocking collectives, per_device_rows(): lax.all_to_all(folded, 'ka', split_axis=0, concat_axis=0, tiled=True)  20.1 us
    pallas_call x1, Pallas kernels, per_device_rows(): pl.pallas_call(fold_kernel, grid=(sites,), in_specs=[pl.BlockSpec((1, wed...  15.1 us
    pallas_call x1, Pallas kernels, per_device_rows(): pl.pallas_call(unfold_kernel, grid=(sites,), in_specs=[pl.BlockSpec((1, O...  13.4 us
    unnamed x19, local copies, waits for them, and re-layouts  11.3 us
    pallas_call x1, Pallas kernels, prepare(): pl.pallas_call(prepare_kernel, grid=(rows // step,), in_specs=[pl.BlockSp...  8.57 us
    all_to_all x1, starting transfers between devices, per_device_rows(): green = lax.all_to_all(green, 'ka', split_axis=0, concat_axis=0, tiled=True)  7.28 us
    all_to_all x1, starting transfers between devices, per_device_rows(): w = lax.all_to_all(sent, 'ka', split_axis=0, concat_axis=0, tiled=True)  4.72 us
  transfers between devices with their start and end apart: 2, of which 2 were waited for; matrix products, arithmetic and copies ran while one was open for 6% of the time, Pallas kernels for 13%

profile of v1, /device:TPU:0, one launch (start us, length us, event | category | flops | bytes accessed | tf_op | source)
XLA Modules:
  0.0 174.1 jit_solution(15498853485451640271)
XLA Ops:
  0.0 0.0 copy-start
  0.0 1.1 copy-done
  1.1 0.8 fusion.10
  1.9 0.9 copy.46
  2.7 7.3 %all-to-all-start = ((bf16[8,1,2,24,768]{4,3,2,1,0:T(8,128)(2,1)}), bf16[8,1,2,24,768]{4,3,2,1,0:T(8,128)(2,1)S(1)}, u32[]{:S(2)}, u32[]{:S(2)}) async-start(bf16[8,1,2,24,768]{4,3,2,1,0:T(8,128)(2,1)} %bitcast.43), calls=%async_computation | async-start | bytes 1179648 | tf_op jit(solution)/shard_map/all_to_all | solution.py:238
  10.0 0.1 fusion.16.swap_ref
  10.1 0.3 fusion.1.order_ref
  10.4 0.0 copy-start.3
  10.4 2.3 %copy-done.3 = bf16[16,192,768]{2,1,0:T(8,128)(2,1)S(1)} copy-done((bf16[16,192,768]{2,1,0:T(8,128)(2,1)S(1)}, bf16[16,192,768]{2,1,0:T(8,128)(2,1)}, u32[]{:S(2)}) %copy-start.3) | copy-done | bytes 4718616
  12.7 8.6 %shard_map.47 = bf16[192,16,768]{2,1,0:T(8,128)(2,1)S(1)} custom-call(bf16[256,256]{1,0:T(8,128)(2,1)S(1)} %fusion.16.swap_ref, bf16[768,768]{1,0:T(8,128)(2,1)S(1)} %fusion.1.order_ref, bf16[16,192,768]{2,1,0:T(8,128)(2,1)S(1)} %copy-done.3), custom_call_target="tpu_custom_call" | custom-call | flops 4800000000 | bytes 9437184 | tf_op jit(solution)/shard_map/pallas_call | solution.py:138
  21.3 0.0 copy-start.1
  21.3 2.2 %copy-done.1 = bf16[192,16,768]{2,1,0:T(8,128)(2,1)} copy-done((bf16[192,16,768]{2,1,0:T(8,128)(2,1)}, bf16[192,16,768]{2,1,0:T(8,128)(2,1)S(1)}, u32[]{:S(2)}) %copy-start.1) | copy-done | bytes 4718616
  23.5 2.4 %all-to-all-done = bf16[8,1,2,24,768]{4,3,2,1,0:T(8,128)(2,1)S(1)} async-done(((bf16[8,1,2,24,768]{4,3,2,1,0:T(8,128)(2,1)}), bf16[8,1,2,24,768]{4,3,2,1,0:T(8,128)(2,1)S(1)}, u32[]{:S(2)}, u32[]{:S(2)}) %all-to-all-start) | async-done | bytes 589856 | tf_op jit(solution)/shard_map/all_to_all | solution.py:238
  25.9 0.0 copy-start.6
  25.9 4.7 %all-to-all-start.1 = ((bf16[8,24,16,768]{3,2,1,0:T(8,128)(2,1)}), bf16[8,24,16,768]{3,2,1,0:T(8,128)(2,1)}, u32[]{:S(2)}, u32[]{:S(2)}) async-start(bf16[8,24,16,768]{3,2,1,0:T(8,128)(2,1)} %bitcast.47), calls=%async_computation.1 | async-start | bytes 9437184 | tf_op jit(solution)/shard_map/all_to_all | solution.py:232
  30.7 0.0 copy-start.7
  30.7 0.0 copy-done.6
  30.7 0.1 fusion.15
  30.8 0.2 copy.30
  30.9 0.1 reshape.208
  31.0 0.3 copy-done.7
  31.4 0.2 copy.31
  31.5 0.1 reshape.209
  31.6 1.0 copy.35
  32.6 0.9 copy.36
  33.5 0.2 convert_reduce_fusion
  33.6 0.1 copy.37.counts_ref
  33.7 0.4 cosine_convert_fusion
  34.1 0.4 fusion.20
  34.5 0.6 pad_maximum_fusion.phase_ref
  35.1 0.1 fusion.13.select_ref
  35.2 1.0 fusion.6.select_ref
  36.2 1.4 fusion.5.coef_ref
  37.6 0.2 copy.33
  37.8 1.4 copy.34
  39.2 2.1 %reshape.213.green_ref = bf16[4,48,1536]{2,1,0:T(8,128)(2,1)S(1)} reshape(bf16[4,8,6,2,768]{4,3,2,1,0:T(2,128)(2,1)} %copy.34) | data formatting | bytes 1179648 | tf_op jit(solution)/shard_map/reshape | solution.py:240
  41.3 0.0 copy-start.2
  41.3 0.8 copy-done.2
  42.2 13.4 %shard_map.46.green_ref = bf16[24,128,768]{2,1,0:T(8,128)(2,1)S(1)} custom-call(bf16[4,768,48]{2,1,0:T(8,128)(2,1)S(1)} %fusion.6.select_ref, bf16[4,48,1536]{2,1,0:T(8,128)(2,1)S(1)} %reshape.213.green_ref, bf16[6,6,128,128]{3,2,1,0:T(8,128)(2,1)S(1)} %fusion.5.coef_ref, bf16[128,256]{1,0:T(8,128)(2,1)S(1)} %copy-done.2), custom_call_target="tpu_custom_call" | custom-call | flops 12000000000 | bytes 12582912 | tf_op jit(solution)/shard_map/pallas_call | solution.py:266
  55.5 0.0 copy-start.4
  55.5 2.2 %copy-done.4 = bf16[24,128,768]{2,1,0:T(8,128)(2,1)} copy-done((bf16[24,128,768]{2,1,0:T(8,128)(2,1)}, bf16[24,128,768]{2,1,0:T(8,128)(2,1)S(1)}, u32[]{:S(2)}) %copy-start.4) | copy-done | bytes 4718616
  57.8 76.6 %all-to-all-done.1.w_ref = bf16[8,24,16,768]{3,2,1,0:T(8,128)(2,1)} async-done(((bf16[8,24,16,768]{3,2,1,0:T(8,128)(2,1)}), bf16[8,24,16,768]{3,2,1,0:T(8,128)(2,1)}, u32[]{:S(2)}, u32[]{:S(2)}) %all-to-all-start.1) | async-done | bytes 4718624 | tf_op jit(solution)/shard_map/all_to_all | solution.py:232
  134.4 0.0 copy-start.5
  134.4 2.3 %copy-done.5 = bf16[24,128,768]{2,1,0:T(8,128)(2,1)S(1)} copy-done((bf16[24,128,768]{2,1,0:T(8,128)(2,1)S(1)}, bf16[24,128,768]{2,1,0:T(8,128)(2,1)}, u32[]{:S(2)}) %copy-start.5) | copy-done | bytes 4718616
  136.7 15.1 %shard_map.48 = bf16[4,48,1536]{2,1,0:T(8,128)(2,1)S(1)} custom-call(bf16[4,48,768]{2,1,0:T(8,128)(2,1)S(1)} %fusion.13.select_ref, f32[48,1]{1,0:T(8,128)S(1)} %copy.37.counts_ref, bf16[24,128,768]{2,1,0:T(8,128)(2,1)S(1)} %copy-done.5, bf16[8,24,16,768]{3,2,1,0:T(8,128)(2,1)} %all-to-all-done.1.w_ref, bf16[6,6,128,128]{3,2,1,0:T(8,128)(2,1)S(1)} %fusion.5.coef_ref, ...), custom_call_target="tpu_custom_call" | custom-call | flops 12000000000 | bytes 12582912 | tf_op jit(solution)/shard_map/pallas_call | solution.py:284
  151.8 0.1 reshape.215
  152.0 0.1 copy.38
  152.0 0.1 copy.39
  152.1 20.1 %all_to_all.15 = bf16[8,1,2,24,768]{4,3,2,1,0:T(8,128)(2,1)S(1)} all-to-all(bf16[8,1,2,24,768]{4,3,2,1,0:T(8,128)(2,1)S(1)} %copy.39), channel_id=1, replica_groups=mesh['ka'=8,'ba'=4] {'ka'}, dimensions={0} | all-to-all | bytes 1179648 | tf_op jit(solution)/shard_map/all_to_all | solution.py:307
  172.3 1.8 %fusion.7 = f32[1,2,192,768]{3,2,1,0:T(8,128)} fusion(bf16[2,192,768]{2,1,0:T(8,128)(2,1)S(1)} %bitcast.53, s32[768]{0:T(1024)S(1)} %fusion.28), kind=kOutput, calls=%fused_computation.9 | convolution fusion | flops 453574656 | bytes 1772544 | tf_op jit(solution)/shard_map/dot_general | solution.py:309
  (14 shorter events, 0.2 us)
Async XLA Ops:
  0.0 1.1 copy-start
  2.7 23.2 %all-to-all-start = ((bf16[8,1,2,24,768]{4,3,2,1,0:T(8,128)(2,1)}), bf16[8,1,2,24,768]{4,3,2,1,0:T(8,128)(2,1)S(1)}, u32[]{:S(2)}, u32[]{:S(2)}) async-start(bf16[8,1,2,24,768]{4,3,2,1,0:T(8,128)(2,1)} %bitcast.43), calls=%async_computation | async-start | bytes 1179648 | tf_op jit(solution)/shard_map/all_to_all | solution.py:238
  10.4 2.3 %copy-start.3 = (bf16[16,192,768]{2,1,0:T(8,128)(2,1)S(1)}, bf16[16,192,768]{2,1,0:T(8,128)(2,1)}, u32[]{:S(2)}) copy-start(bf16[16,192,768]{2,1,0:T(8,128)(2,1)} %w_ref.1) | copy-start | bytes 14155780
  21.3 2.2 %copy-start.1 = (bf16[192,16,768]{2,1,0:T(8,128)(2,1)}, bf16[192,16,768]{2,1,0:T(8,128)(2,1)S(1)}, u32[]{:S(2)}) copy-start(bf16[192,16,768]{2,1,0:T(8,128)(2,1)S(1)} %shard_map.47) | copy-start | bytes 14155780
  25.9 4.8 %copy-start.6 = (s32[128,768]{1,0:T(8,128)S(1)}, s32[128,768]{1,0:T(8,128)}, u32[]{:S(2)}) copy-start(s32[128,768]{1,0:T(8,128)} %param.7) | copy-start | bytes 1179652
  25.9 108.5 %all-to-all-start.1 = ((bf16[8,24,16,768]{3,2,1,0:T(8,128)(2,1)}), bf16[8,24,16,768]{3,2,1,0:T(8,128)(2,1)}, u32[]{:S(2)}, u32[]{:S(2)}) async-start(bf16[8,24,16,768]{3,2,1,0:T(8,128)(2,1)} %bitcast.47), calls=%async_computation.1 | async-start | bytes 9437184 | tf_op jit(solution)/shard_map/all_to_all | solution.py:232
  30.7 0.7 copy-start.7
  41.3 0.8 copy-start.2
  55.5 2.2 %copy-start.4 = (bf16[24,128,768]{2,1,0:T(8,128)(2,1)}, bf16[24,128,768]{2,1,0:T(8,128)(2,1)S(1)}, u32[]{:S(2)}) copy-start(bf16[24,128,768]{2,1,0:T(8,128)(2,1)S(1)} %shard_map.46.green_ref) | copy-start | bytes 14155780
  134.4 2.3 %copy-start.5 = (bf16[24,128,768]{2,1,0:T(8,128)(2,1)S(1)}, bf16[24,128,768]{2,1,0:T(8,128)(2,1)}, u32[]{:S(2)}) copy-start(bf16[24,128,768]{2,1,0:T(8,128)(2,1)} %copy-done.4) | copy-start | bytes 14155780

commit v2 on v1

--- a/solution.py
+++ b/solution.py
@@ -5,6 +5,7 @@
 from jax import lax
 from jax.experimental import pallas as pl
 from jax.experimental.pallas import tpu as pltpu
+from jax.sharding import Mesh
 from jax.sharding import PartitionSpec as P
 
 KX = 8
@@ -122,29 +123,38 @@
     return (moved[:, None] == place[None, :]).astype(jnp.bfloat16)
 
 
-def prepare_kernel(swap_ref, order_ref, w_ref, out_ref):
+def prepare_kernel(swap_ref, order_ref, w_ref, *out_refs):
     count, rows, basis = w_ref.shape
-    block = w_ref[...].reshape(count * rows, basis)
-    turned = jnp.dot(swap_ref[...], block, preferred_element_type=jnp.float32).astype(jnp.bfloat16)
-    out = jnp.dot(turned, order_ref[...], preferred_element_type=jnp.float32).astype(jnp.bfloat16)
-    out_ref[...] = out.reshape(rows, count, basis)
-
-
-def prepare(screened, order, step=16):
+    step = swap_ref.shape[0] // count
+    each = rows // len(out_refs)
+    for start in range(0, rows, step):
+        block = w_ref[:, start : start + step, :].reshape(count * step, basis)
+        turned = jnp.dot(swap_ref[...], block, preferred_element_type=jnp.float32)
+        out = jnp.dot(
+            turned.astype(jnp.bfloat16), order_ref[...], preferred_element_type=jnp.float32
+        ).astype(jnp.bfloat16)
+        out = out.reshape(step, count, basis)
+        for row in range(start, start + step):
+            out_refs[row // each][0, row % each] = out[row - start]
+
+
+def prepare(screened, order, width, pieces, step=16):
     count, rows, basis = screened.shape
+    part = rows // width
+    each = part // pieces
     place = jnp.arange(count * step, dtype=jnp.int32)
     origin = (place % count) * step + place // count
     swap = (origin[:, None] == place[None, :]).astype(jnp.bfloat16)
     return pl.pallas_call(
         prepare_kernel,
-        grid=(rows // step,),
+        grid=(width,),
         in_specs=[
             pl.BlockSpec((count * step, count * step), lambda i: (0, 0)),
             pl.BlockSpec((basis, basis), lambda i: (0, 0)),
-            pl.BlockSpec((count, step, basis), lambda i: (0, i, 0)),
+            pl.BlockSpec((count, part, basis), lambda i: (0, i, 0)),
         ],
-        out_specs=pl.BlockSpec((step, count, basis), lambda i: (i, 0, 0)),
-        out_shape=jax.ShapeDtypeStruct((rows, count, basis), jnp.bfloat16),
+        out_specs=[pl.BlockSpec((1, each, count, basis), lambda i: (i, 0, 0, 0))] * pieces,
+        out_shape=[jax.ShapeDtypeStruct((width, each, count, basis), jnp.bfloat16)] * pieces,
         compiler_params=pltpu.CompilerParams(vmem_limit_bytes=24 << 20),
         cost_estimate=pl.CostEstimate(
             flops=4800000000, bytes_accessed=4 * count * rows * basis, transcendentals=0
@@ -171,7 +181,7 @@
 
 
 def unfold_kernel(select_ref, green_ref, coef_ref, phase_ref, out_ref, half, full):
-    zone = phase_ref.shape[0]
+    zone = phase_ref.shape[1] // 2
     basis = out_ref.shape[2]
     atoms = basis // ORB
     half[...] = jnp.dot(select_ref[0], green_ref[0], preferred_element_type=jnp.float32).astype(
@@ -193,11 +203,12 @@
 
 
 def fold_kernel(select_ref, counts_ref, green_ref, w_ref, coef_ref, phase_ref, out_ref, full, half):
-    zone = phase_ref.shape[1]
+    near = phase_ref.shape[1]
+    zone = phase_ref.shape[0] // 2
     basis = green_ref.shape[2]
     atoms = basis // ORB
     for oa in range(ORB):
-        w = w_ref[:, oa].reshape(zone, basis)
+        w = w_ref[:, oa].reshape(near, basis)
         sigma = (-(green_ref[oa].astype(jnp.float32) * w.astype(jnp.float32))).astype(jnp.bfloat16)
         full[oa] = jnp.dot(phase_ref[...], sigma, preferred_element_type=jnp.float32).astype(
             jnp.bfloat16
@@ -216,30 +227,45 @@
     out_ref[0] = (sums / counts_ref[...]).astype(jnp.bfloat16)
 
 
+PIECES = 2
+HALVES = 2
+
+
 def per_device_rows(green_irr, screened, kmap, rotation):
-    width = lax.axis_size("ka")
+    halves = lax.axis_size("kh")
+    width = lax.axis_size("kl")
+    both = ("kh", "kl")
     zone, basis = rotation.shape
     atoms = basis // ORB
     own, _, rows, _ = green_irr.shape
-    wedges = own * width
+    wedges = own * width * halves
     part = rows // width
     sites = part // ORB
+    each = part // PIECES
+    group = sites // PIECES
     near = screened.shape[0]
+    here = near * width
     targets = kmap[:, 0]
     order = column_order(basis)
 
-    sent = prepare(screened, order).reshape(width, part, near, basis)
-    w = lax.all_to_all(sent, "ka", split_axis=0, concat_axis=0, tiled=True)
+    sent = prepare(screened, order, width, PIECES)
+    w = [lax.all_to_all(x, "kl", split_axis=0, concat_axis=0, tiled=True) for x in sent]
 
     green = jnp.dot(
         green_irr.reshape(own * 2 * rows, basis), order, preferred_element_type=jnp.float32
     ).astype(jnp.bfloat16)
     green = green.reshape(own, 2, width, part, basis).transpose(2, 0, 1, 3, 4)
-    green = lax.all_to_all(green, "ka", split_axis=0, concat_axis=0, tiled=True)
+    green = jnp.concatenate([green] * halves, axis=0)
+    green = lax.all_to_all(green, both, split_axis=0, concat_axis=0, tiled=True)
     green = green.reshape(wedges, 2, sites, ORB, basis).transpose(2, 0, 3, 1, 4)
     green = green.reshape(sites, wedges * ORB, 2 * basis)
 
     cos_t, sin_t = phase_tables(zone)
+    first_r = lax.axis_index("kh") * here
+    forth = jnp.concatenate([cos_t, -sin_t], axis=1)
+    forth = lax.dynamic_slice_in_dim(forth, first_r, here, 0)
+    back_t = jnp.concatenate([cos_t, -sin_t], axis=0)
+    back_t = lax.dynamic_slice_in_dim(back_t, first_r, here, 1)
     source, signs = decode(rotation)
     orbital = jnp.arange(ORB, dtype=jnp.int32)
     place = source - (jnp.arange(basis, dtype=jnp.int32) // ORB * ORB)[None, :]
@@ -247,7 +273,7 @@
     sign = signs.reshape(zone, atoms, ORB).transpose(2, 0, 1)
     coef = (place[:, None] == orbital[None, :, None, None]).astype(jnp.bfloat16) * sign[:, None]
 
-    first = lax.axis_index("ba") * rows // ORB + lax.axis_index("ka") * sites
+    first = lax.axis_index("ba") * rows // ORB + lax.axis_index("kl") * sites
     row_place = lax.dynamic_slice_in_dim(place, first, sites, 2).transpose(2, 0, 1)
     row_sign = lax.dynamic_slice_in_dim(sign, first, sites, 2).transpose(2, 0, 1)
     code = targets[None, None, :] * ORB + row_place
@@ -262,7 +288,7 @@
 
     whole = lambda shape: pl.BlockSpec(shape, lambda i: (0,) * len(shape))
     params = pltpu.CompilerParams(vmem_limit_bytes=40 << 20)
-    cost = pl.CostEstimate(flops=12000000000, bytes_accessed=12 << 20, transcendentals=0)
+    cost = pl.CostEstimate(flops=20000000000, bytes_accessed=12 << 20, transcendentals=0)
     green_r = pl.pallas_call(
         unfold_kernel,
         grid=(sites,),
@@ -270,58 +296,82 @@
             pl.BlockSpec((1, ORB * zone, wedges * ORB), lambda i: (i, 0, 0)),
             pl.BlockSpec((1, wedges * ORB, 2 * basis), lambda i: (i, 0, 0)),
             whole(coef.shape),
-            whole((zone, 2 * zone)),
+            whole(forth.shape),
         ],
-        out_specs=pl.BlockSpec((ORB, zone, basis), lambda i: (i, 0, 0)),
-        out_shape=jax.ShapeDtypeStruct((part, zone, basis), jnp.bfloat16),
+        out_specs=pl.BlockSpec((ORB, here, basis), lambda i: (i, 0, 0)),
+        out_shape=jax.ShapeDtypeStruct((part, here, basis), jnp.bfloat16),
         scratch_shapes=[
             pltpu.VMEM((ORB * zone, 2 * basis), jnp.bfloat16),
             pltpu.VMEM((ORB, 2 * zone, basis), jnp.bfloat16),
         ],
         compiler_params=params,
         cost_estimate=cost,
-    )(select, green, coef, jnp.concatenate([cos_t, -sin_t], axis=1))
-    folded = pl.pallas_call(
-        fold_kernel,
-        grid=(sites,),
-        in_specs=[
-            pl.BlockSpec((1, wedges * ORB, ORB * zone), lambda i: (i, 0, 0)),
-            whole((wedges * ORB, 1)),
-            pl.BlockSpec((ORB, zone, basis), lambda i: (i, 0, 0)),
-            pl.BlockSpec((width, ORB, near, basis), lambda i: (0, i, 0, 0)),
-            whole(coef.shape),
-            whole((2 * zone, zone)),
-        ],
-        out_specs=pl.BlockSpec((1, wedges * ORB, 2 * basis), lambda i: (i, 0, 0)),
-        out_shape=jax.ShapeDtypeStruct((sites, wedges * ORB, 2 * basis), jnp.bfloat16),
-        scratch_shapes=[
-            pltpu.VMEM((ORB, 2 * zone, basis), jnp.bfloat16),
-            pltpu.VMEM((ORB * zone, 2 * basis), jnp.bfloat16),
-        ],
-        compiler_params=params,
-        cost_estimate=cost,
-    )(back, counts, green_r, w, coef, jnp.concatenate([cos_t, -sin_t], axis=0))
-
-    folded = folded.reshape(sites, wedges, ORB, 2, basis).transpose(1, 3, 0, 2, 4)
-    folded = folded.reshape(width, own, 2, part, basis)
-    folded = lax.all_to_all(folded, "ka", split_axis=0, concat_axis=0, tiled=True)
-    folded = folded.transpose(1, 2, 0, 3, 4).reshape(own * 2 * rows, basis)
-    out = lax.dot_general(
-        folded, order, (((1,), (1,)), ((), ())), preferred_element_type=jnp.float32
-    )
+    )(select, green, coef, forth)
+
+    outs = []
+    for piece in range(PIECES):
+        skip = piece * group
+        folded = pl.pallas_call(
+            fold_kernel,
+            grid=(group,),
+            in_specs=[
+                pl.BlockSpec((1, wedges * ORB, ORB * zone), lambda i, s=skip: (i + s, 0, 0)),
+                whole((wedges * ORB, 1)),
+                pl.BlockSpec((ORB, here, basis), lambda i, s=skip: (i + s, 0, 0)),
+                pl.BlockSpec((width, ORB, near, basis), lambda i: (0, i, 0, 0)),
+                whole(coef.shape),
+                whole(back_t.shape),
+            ],
+            out_specs=pl.BlockSpec((1, wedges * ORB, 2 * basis), lambda i: (i, 0, 0)),
+            out_shape=jax.ShapeDtypeStruct((group, wedges * ORB, 2 * basis), jnp.bfloat16),
+            scratch_shapes=[
+                pltpu.VMEM((ORB, 2 * zone, basis), jnp.bfloat16),
+                pltpu.VMEM((ORB * zone, 2 * basis), jnp.bfloat16),
+            ],
+            compiler_params=params,
+            cost_estimate=cost,
+        )(back, counts, green_r, w[piece], coef, back_t)
+        folded = folded.reshape(group, wedges, ORB, 2, basis).transpose(1, 3, 0, 2, 4)
+        folded = folded.reshape(width * halves, own, 2, each, basis)
+        folded = lax.all_to_all(folded, both, split_axis=0, concat_axis=0, tiled=True)
+        folded = folded.reshape(halves, width * own * 2 * each, basis)
+        out = sum(
+            lax.dot_general(
+                folded[h], order, (((1,), (1,)), ((), ())), preferred_element_type=jnp.float32
+            )
+            for h in range(halves)
+        )
+        outs.append(out.reshape(width, own, 2, each, basis))
+    out = jnp.stack(outs, axis=1).transpose(2, 3, 0, 1, 4, 5)
     return out.reshape(own, 2, rows, basis)
 
 
-def per_device(green_irr, screened, kmap, rotation):
-    rows = green_irr.shape[2]
-    width = lax.axis_size("ka")
-    if rows % (width * ORB) == 0 and screened.shape[0] % 16 == 0:
-        return per_device_rows(green_irr, screened, kmap, rotation)
-    return per_device_columns(green_irr, screened, kmap, rotation)
-
-
 def solution(mesh):
-    placed = (P("ka", None, "ba", None), P("ka", "ba", None), P(), P())
-    return jax.shard_map(
-        per_device, mesh=mesh, in_specs=placed, out_specs=P("ka", None, "ba", None), check_vma=False
-    )
+    sizes = mesh.shape
+    width, lines = sizes["ka"], sizes["ba"]
+    columns = (P("ka", None, "ba", None), P("ka", "ba", None), P(), P())
+
+    def run(green_irr, screened, kmap, rotation):
+        rows = green_irr.shape[2] // lines
+        near = screened.shape[0] // width
+        parts = width // HALVES
+        if width % HALVES or rows % (parts * ORB * PIECES) or rows // parts % 16 or near % 16:
+            return jax.shard_map(
+                per_device_columns,
+                mesh=mesh,
+                in_specs=columns,
+                out_specs=P("ka", None, "ba", None),
+                check_vma=False,
+            )(green_irr, screened, kmap, rotation)
+        finer = Mesh(mesh.devices.reshape(HALVES, parts, lines), ("kh", "kl", "ba"))
+        both = ("kh", "kl")
+        placed = (P(both, None, "ba", None), P(both, "ba", None), P(), P())
+        return jax.shard_map(
+            per_device_rows,
+            mesh=finer,
+            in_specs=placed,
+            out_specs=P(both, None, "ba", None),
+            check_vma=False,
+        )(green_irr, screened, kmap, rotation)
+
+    return run

time: 175 us -> 178 us (1.017)
  waiting for transfers between devices: 79 us -> 30.5 us
  Pallas kernels: 37 us -> 62.9 us
  local copies, waits for them, and re-layouts: 18.5 us -> 40.2 us
  blocking collectives: 20.1 us -> 0 us
  starting transfers between devices: 12 us -> 25.8 us
  other arithmetic: 4.51 us -> 13.4 us
    all_to_all x2 -> x5, waiting for transfers between devices: 79 us -> 30.5 us  [the longest x1 17.2 us: per_device_rows(): green = lax.all_to_all(green, both, split_axis=0, concat_axis=0, tiled=True)]
    all_to_all x1 -> x0, blocking collectives: 20.1 us -> none  [per_device_rows(): lax.all_to_all(folded, 'ka', split_axis=0, concat_axis=0, tiled=True)]
    all_to_all x2 -> x5, starting transfers between devices: 12 us -> 25.8 us  [the longest x2 10.2 us: per_device_rows(): lax.all_to_all(folded, both, split_axis=0, concat_axis=0, tiled=True)]
    pallas_call x1, Pallas kernels: 13.4 us -> 27.1 us  [per_device_rows(): pl.pallas_call(unfold_kernel, grid=(sites,), in_specs=[pl.BlockSpec((1, O...]
    pallas_call x2 -> x3, Pallas kernels: 23.6 us -> 35.8 us  [the longest x2 28.6 us: per_device_rows(): pl.pallas_call(fold_kernel, grid=(group,), in_specs=[pl.BlockSpec((1, wed...]
    unnamed x19 -> x45, local copies, waits for them, and re-layouts: 11.3 us -> 17.3 us
    reshape x3 -> x6, local copies, waits for them, and re-layouts: 0.3 us -> 4.06 us  [the longest x4 2.22 us: per_device_rows(): folded.reshape(group, wedges, ORB, 2, basis).transpose(1, 3, 0, 2, 4)]
    mul x1, other arithmetic: 1.05 us -> 4.69 us  [per_device_rows(): (code[:, :, None] == hit[None, None, :]).astype(jnp.bfloat16)]
  transfers between devices with their start and end apart: 2 -> 5, of which waited for: 2 -> 2; matrix products, arithmetic and copies ran while one was open for 6% -> 20% of each run, Pallas kernels for 13% -> 36%
where the time goes in v2:
time: 178 us; the launch traced here: 177 us
  Pallas kernels  62.9 us (35%)
  local copies, waits for them, and re-layouts  40.2 us (23%)
  waiting for transfers between devices  30.5 us (17%)
  starting transfers between devices  25.8 us (14%)
  other arithmetic  13.4 us (8%)
  matrix products  3.6 us (2%)
    pallas_call x2, Pallas kernels, per_device_rows(): pl.pallas_call(fold_kernel, grid=(group,), in_specs=[pl.BlockSpec((1, wed...  28.6 us
    pallas_call x1, Pallas kernels, per_device_rows(): pl.pallas_call(unfold_kernel, grid=(sites,), in_specs=[pl.BlockSpec((1, O...  27.1 us
    unnamed x45, local copies, waits for them, and re-layouts  17.3 us
    all_to_all x1, waiting for transfers between devices, per_device_rows(): green = lax.all_to_all(green, both, split_axis=0, concat_axis=0, tiled=True)  17.2 us
    all_to_all x2, waiting for transfers between devices, per_device_rows(): lax.all_to_all(folded, both, split_axis=0, concat_axis=0, tiled=True)  13.3 us
    all_to_all x2, starting transfers between devices, per_device_rows(): lax.all_to_all(folded, both, split_axis=0, concat_axis=0, tiled=True)  10.2 us
    all_to_all x2, starting transfers between devices, per_device_rows(): lax.all_to_all(x, 'kl', split_axis=0, concat_axis=0, tiled=True)  8.31 us
    all_to_all x1, starting transfers between devices, per_device_rows(): green = lax.all_to_all(green, both, split_axis=0, concat_axis=0, tiled=True)  7.28 us
  transfers between devices with their start and end apart: 5, of which 2 were waited for; matrix products, arithmetic and copies ran while one was open for 20% of the time, Pallas kernels for 36%

profile of v2, /device:TPU:0, one launch (start us, length us, event | category | flops | bytes accessed | tf_op | source)
XLA Modules:
  0.0 176.7 jit_solution(14858225523660179267)
XLA Ops:
  0.0 1.1 copy-done
  1.1 0.8 fusion.8
  1.9 1.1 pad_maximum_fusion
  3.1 7.3 %all-to-all-start = ((bf16[8,1,2,48,768]{4,3,2,1,0:T(8,128)(2,1)}), bf16[8,1,2,48,768]{4,3,2,1,0:T(8,128)(2,1)S(1)}, u32[]{:S(2)}, u32[]{:S(2)}) async-start(bf16[8,1,2,48,768]{4,3,2,1,0:T(8,128)(2,1)} %pad_maximum_fusion), calls=%async_computation | async-start | bytes 2359296 | tf_op jit(solution)/shard_map/all_to_all | solution.py:259
  10.3 0.1 fusion.19.swap_ref
  10.5 0.3 fusion.5.order_ref
  10.7 2.3 %copy-done.12 = bf16[16,192,768]{2,1,0:T(8,128)(2,1)S(1)} copy-done((bf16[16,192,768]{2,1,0:T(8,128)(2,1)S(1)}, bf16[16,192,768]{2,1,0:T(8,128)(2,1)}, u32[]{:S(2)}) %copy-start.12) | copy-done | bytes 4718616
  13.1 7.2 %shard_map.47 = (bf16[4,24,16,768]{3,2,1,0:T(8,128)(2,1)S(1)}, bf16[4,24,16,768]{3,2,1,0:T(8,128)(2,1)}) custom-call(bf16[256,256]{1,0:T(8,128)(2,1)S(1)} %fusion.19.swap_ref, bf16[768,768]{1,0:T(8,128)(2,1)S(1)} %fusion.5.order_ref, bf16[16,192,768]{2,1,0:T(8,128)(2,1)S(1)} %copy-done.12), custom_call_target="tpu_custom_call" | custom-call | flops 4800000000 | bytes 9437184 | tf_op jit(solution)/shard_map/pallas_call | solution.py:148
  20.3 1.4 copy-done.1
  21.7 17.2 %all-to-all-done = bf16[8,1,2,48,768]{4,3,2,1,0:T(8,128)(2,1)S(1)} async-done(((bf16[8,1,2,48,768]{4,3,2,1,0:T(8,128)(2,1)}), bf16[8,1,2,48,768]{4,3,2,1,0:T(8,128)(2,1)S(1)}, u32[]{:S(2)}, u32[]{:S(2)}) %all-to-all-start) | async-done | bytes 1179680 | tf_op jit(solution)/shard_map/all_to_all | solution.py:259
  38.9 1.0 copy-done.15
  39.9 3.6 %all-to-all-start.1 = ((bf16[4,24,16,768]{3,2,1,0:T(8,128)(2,1)}), bf16[4,24,16,768]{3,2,1,0:T(8,128)(2,1)S(1)}, u32[]{:S(2)}, u32[]{:S(2)}) async-start(bf16[4,24,16,768]{3,2,1,0:T(8,128)(2,1)} %copy-done.1), calls=%async_computation.1 | async-start | bytes 4718592 | tf_op jit(solution)/shard_map/all_to_all | solution.py:252
  43.6 0.0 copy-start.20
  43.6 0.8 fusion.18
  44.5 1.9 %copy.56 = s32[128,768]{0,1:T(8,128)} copy(s32[128,768]{1,0:T(8,128)} %fusion.18) | data formatting | bytes 786432 | tf_op jit(solution)/shard_map/sub | solution.py:271
  46.4 1.0 reshape.215
  47.5 0.6 copy.80
  48.1 1.7 fusion.17
  49.8 1.7 copy.57
  51.5 1.7 reshape.216
  53.2 0.7 dynamic-slice_bitcast_fusion
  54.0 1.0 copy.61
  54.9 1.8 %copy.62 = bf16[6,128,128]{2,1,0:T(8,128)(2,1)} copy(bf16[6,128,128]{1,0,2:T(8,128)(2,1)} %bitcast.62) | data formatting | bytes 393216 | tf_op jit(solution)/shard_map/transpose | solution.py:273
  56.8 0.2 convert_reduce_fusion
  56.9 0.7 copy.63.counts_ref
  57.7 0.4 cosine_convert_fusion
  58.0 0.4 fusion.23
  58.4 0.6 fusion.24.phase_ref
  59.0 0.7 dynamic-slice_maximum_fusion.phase_ref
  59.7 0.9 fusion.16.select_ref
  60.6 0.0 copy-start.16
  60.6 4.7 %fusion.select_ref = bf16[8,768,48]{2,1,0:T(8,128)(2,1)} fusion(s32[8,768]{1,0:T(8,128)} %bitcast.71, bf16[8,768]{1,0:T(8,128)(2,1)S(1)} %bitcast.73), kind=kLoop, calls=%fused_computation.1 | loop fusion | flops 589824 | bytes 626688 | tf_op jit(solution)/shard_map/mul | solution.py:283
  65.3 1.4 fusion.7.coef_ref
  66.7 0.7 copy.59
  67.4 2.2 %copy.60 = bf16[8,8,6,2,768]{4,3,2,1,0:T(2,128)(2,1)} copy(bf16[8,8,6,2,768]{4,1,2,0,3:T(8,128)(2,1)S(1)} %bitcast.56) | data formatting | bytes 2359296 | tf_op jit(solution)/shard_map/transpose | solution.py:260
  69.6 3.8 %reshape.220.green_ref = bf16[8,48,1536]{2,1,0:T(8,128)(2,1)} reshape(bf16[8,8,6,2,768]{4,3,2,1,0:T(2,128)(2,1)} %copy.60) | data formatting | bytes 2359296 | tf_op jit(solution)/shard_map/reshape | solution.py:261
  73.5 4.7 %all-to-all-start.3 = ((bf16[4,24,16,768]{3,2,1,0:T(8,128)(2,1)}), bf16[4,24,16,768]{3,2,1,0:T(8,128)(2,1)}, u32[]{:S(2)}, u32[]{:S(2)}) async-start(bf16[4,24,16,768]{3,2,1,0:T(8,128)(2,1)} %get-tuple-element.8), calls=%async_computation.3 | async-start | bytes 4718592 | tf_op jit(solution)/shard_map/all_to_all | solution.py:252
  78.1 1.4 copy-done.2
  79.5 1.3 copy-done.3
  80.8 1.3 copy-done.5
  82.1 0.8 copy-done.9
  82.9 27.1 %shard_map.46.green_ref = bf16[48,64,768]{2,1,0:T(8,128)(2,1)S(1)} custom-call(bf16[8,768,48]{2,1,0:T(8,128)(2,1)S(1)} %copy-done.2, bf16[8,48,1536]{2,1,0:T(8,128)(2,1)S(1)} %copy-done.5, bf16[6,6,128,128]{3,2,1,0:T(8,128)(2,1)S(1)} %copy-done.3, bf16[64,256]{1,0:T(8,128)(2,1)S(1)} %copy-done.9), custom_call_target="tpu_custom_call" | custom-call | flops 20000000000 | bytes 12582912 | tf_op jit(solution)/shard_map/pallas_call | solution.py:292
  110.0 13.8 %shard_map.48 = bf16[4,48,1536]{2,1,0:T(8,128)(2,1)S(1)} custom-call(bf16[8,48,768]{2,1,0:T(8,128)(2,1)S(1)} %fusion.16.select_ref, f32[48,1]{1,0:T(8,128)S(1)} %copy-done.10, bf16[48,64,768]{2,1,0:T(8,128)(2,1)S(1)} %shard_map.46.green_ref, bf16[4,24,16,768]{3,2,1,0:T(8,128)(2,1)S(1)} %all-to-all-done.1.w_ref, bf16[6,6,128,128]{3,2,1,0:T(8,128)(2,1)S(1)} %copy-done.3, ...), custom_call_target="tpu_custom_call" | custom-call | flops 20000000000 | bytes 12582912 | tf_op jit(solution)/shard_map/pallas_call | solution.py:314
  123.8 0.0 copy-start.6
  123.8 0.8 copy-done.6
  124.6 2.2 %copy-done.13 = bf16[48,64,768]{2,1,0:T(8,128)(2,1)} copy-done((bf16[48,64,768]{2,1,0:T(8,128)(2,1)}, bf16[48,64,768]{2,1,0:T(8,128)(2,1)S(1)}, u32[]{:S(2)}) %copy-start.13) | copy-done | bytes 4718616
  126.8 2.0 %reshape.221 = bf16[4,8,6,2,768]{4,3,2,1,0:T(2,128)(2,1)S(1)} reshape(bf16[4,48,1536]{2,1,0:T(8,128)(2,1)} %copy-done.6) | data formatting | bytes 1179648 | tf_op jit(solution)/shard_map/reshape | solution.py:334
  128.8 0.1 copy.64
  128.9 0.9 copy.65
  129.8 4.2 %all-to-all-start.2 = ((bf16[8,1,2,24,768]{4,3,2,1,0:T(8,128)(2,1)}), bf16[8,1,2,24,768]{4,3,2,1,0:T(8,128)(2,1)}, u32[]{:S(2)}, u32[]{:S(2)}) async-start(bf16[8,1,2,24,768]{4,3,2,1,0:T(8,128)(2,1)} %copy.65), calls=%async_computation.2 | async-start | bytes 1179648 | tf_op jit(solution)/shard_map/all_to_all | solution.py:336
  134.1 2.3 %copy-done.14 = bf16[48,64,768]{2,1,0:T(8,128)(2,1)S(1)} copy-done((bf16[48,64,768]{2,1,0:T(8,128)(2,1)S(1)}, bf16[48,64,768]{2,1,0:T(8,128)(2,1)}, u32[]{:S(2)}) %copy-start.14) | copy-done | bytes 4718616
  136.4 14.8 %shard_map.49 = bf16[4,48,1536]{2,1,0:T(8,128)(2,1)S(1)} custom-call(bf16[8,48,768]{2,1,0:T(8,128)(2,1)S(1)} %fusion.16.select_ref, f32[48,1]{1,0:T(8,128)S(1)} %copy-done.11, bf16[48,64,768]{2,1,0:T(8,128)(2,1)S(1)} %copy-done.14, bf16[4,24,16,768]{3,2,1,0:T(8,128)(2,1)} %all-to-all-done.3.w_ref, bf16[6,6,128,128]{3,2,1,0:T(8,128)(2,1)S(1)} %copy-done.4, ...), custom_call_target="tpu_custom_call" | custom-call | flops 20000000000 | bytes 12582912 | tf_op jit(solution)/shard_map/pallas_call | solution.py:314
  151.2 0.1 reshape.223
  151.3 0.1 copy.69
  151.4 0.9 copy.70
  152.3 6.0 %all-to-all-start.4 = ((bf16[8,1,2,24,768]{4,3,2,1,0:T(8,128)(2,1)}), bf16[8,1,2,24,768]{4,3,2,1,0:T(8,128)(2,1)S(1)}, u32[]{:S(2)}, u32[]{:S(2)}) async-start(bf16[8,1,2,24,768]{4,3,2,1,0:T(8,128)(2,1)} %copy.70), calls=%async_computation.4 | async-start | bytes 1179648 | tf_op jit(solution)/shard_map/all_to_all | solution.py:336
  158.3 1.1 fusion.39
  159.4 0.7 fusion.3
  160.1 13.3 %all-to-all-done.4 = bf16[8,1,2,24,768]{4,3,2,1,0:T(8,128)(2,1)S(1)} async-done(((bf16[8,1,2,24,768]{4,3,2,1,0:T(8,128)(2,1)}), bf16[8,1,2,24,768]{4,3,2,1,0:T(8,128)(2,1)S(1)}, u32[]{:S(2)}, u32[]{:S(2)}) %all-to-all-start.4) | async-done | bytes 589856 | tf_op jit(solution)/shard_map/all_to_all | solution.py:336
  173.4 0.7 fusion.1
  174.1 0.7 fusion.9
  174.8 0.7 fusion.10
  175.5 0.1 maximum_bitcast_fusion
  175.6 1.1 copy.73
  (42 shorter events, 0.2 us)
Async XLA Ops:
  0.0 1.1 copy-start
  3.1 35.9 %all-to-all-start = ((bf16[8,1,2,48,768]{4,3,2,1,0:T(8,128)(2,1)}), bf16[8,1,2,48,768]{4,3,2,1,0:T(8,128)(2,1)S(1)}, u32[]{:S(2)}, u32[]{:S(2)}) async-start(bf16[8,1,2,48,768]{4,3,2,1,0:T(8,128)(2,1)} %pad_maximum_fusion), calls=%async_computation | async-start | bytes 2359296 | tf_op jit(solution)/shard_map/all_to_all | solution.py:259
  10.7 2.3 %copy-start.12 = (bf16[16,192,768]{2,1,0:T(8,128)(2,1)S(1)}, bf16[16,192,768]{2,1,0:T(8,128)(2,1)}, u32[]{:S(2)}) copy-start(bf16[16,192,768]{2,1,0:T(8,128)(2,1)} %w_ref.1) | copy-start | bytes 14155780
  20.3 1.4 copy-start.1
  38.9 1.0 copy-start.15
  38.9 4.7 %copy-start.18 = (s32[128,768]{1,0:T(8,128)S(1)}, s32[128,768]{1,0:T(8,128)}, u32[]{:S(2)}) copy-start(s32[128,768]{1,0:T(8,128)} %param.7) | copy-start | bytes 1179652
  39.9 33.5 %all-to-all-start.1 = ((bf16[4,24,16,768]{3,2,1,0:T(8,128)(2,1)}), bf16[4,24,16,768]{3,2,1,0:T(8,128)(2,1)S(1)}, u32[]{:S(2)}, u32[]{:S(2)}) async-start(bf16[4,24,16,768]{3,2,1,0:T(8,128)(2,1)} %copy-done.1), calls=%async_computation.1 | async-start | bytes 4718592 | tf_op jit(solution)/shard_map/all_to_all | solution.py:252
  43.6 3.9 %copy-start.20 = (s32[128,1]{0,1:T(1,128)S(1)}, s32[128,1]{0,1:T(1,128)}, u32[]{:S(2)}) copy-start(s32[128,1]{0,1:T(1,128)} %param.6) | copy-start | bytes 1540
  57.6 7.7 %copy-start.17 = (s32[6,128,128]{2,1,0:T(8,128)S(1)}, s32[6,128,128]{2,1,0:T(8,128)}, u32[]{:S(2)}) copy-start(s32[6,128,128]{2,1,0:T(8,128)} %copy.61) | copy-start | bytes 1179652
  57.7 7.7 %copy-start.19 = (bf16[6,128,128]{2,1,0:T(8,128)(2,1)S(1)}, bf16[6,128,128]{2,1,0:T(8,128)(2,1)}, u32[]{:S(2)}) copy-start(bf16[6,128,128]{2,1,0:T(8,128)(2,1)} %copy.62) | copy-start | bytes 589828
  60.6 6.1 %copy-start.16 = (bf16[8,1,2,48,768]{4,3,2,1,0:T(8,128)(2,1)S(1)}, bf16[8,1,2,48,768]{4,3,2,1,0:T(8,128)(2,1)}, u32[]{:S(2)}) copy-start(bf16[8,1,2,48,768]{4,3,2,1,0:T(8,128)(2,1)} %copy-done.15) | copy-start | bytes 3538948
  73.5 56.4 %all-to-all-start.3 = ((bf16[4,24,16,768]{3,2,1,0:T(8,128)(2,1)}), bf16[4,24,16,768]{3,2,1,0:T(8,128)(2,1)}, u32[]{:S(2)}, u32[]{:S(2)}) async-start(bf16[4,24,16,768]{3,2,1,0:T(8,128)(2,1)} %get-tuple-element.8), calls=%async_computation.3 | async-start | bytes 4718592 | tf_op jit(solution)/shard_map/all_to_all | solution.py:252
  78.1 1.4 copy-start.2
  79.5 1.3 copy-start.3
  80.8 1.3 copy-start.5
  82.1 0.8 copy-start.9
  82.8 27.1 %copy-start.7 = (bf16[256,64]{1,0:T(8,128)(2,1)S(1)}, bf16[256,64]{1,0:T(8,128)(2,1)}, u32[]{:S(2)}) copy-start(bf16[256,64]{1,0:T(8,128)(2,1)} %dynamic-slice_maximum_fusion.phase_ref) | copy-start | bytes 98308
  82.9 27.1 %copy-start.10 = (f32[48,1]{1,0:T(8,128)S(1)}, f32[48,1]{1,0:T(8,128)}, u32[]{:S(2)}) copy-start(f32[48,1]{1,0:T(8,128)} %copy.63.counts_ref) | copy-start | bytes 580
  123.8 0.8 copy-start.6
  124.6 2.2 %copy-start.13 = (bf16[48,64,768]{2,1,0:T(8,128)(2,1)}, bf16[48,64,768]{2,1,0:T(8,128)(2,1)S(1)}, u32[]{:S(2)}) copy-start(bf16[48,64,768]{2,1,0:T(8,128)(2,1)S(1)} %shard_map.46.green_ref) | copy-start | bytes 14155780
  128.8 5.2 %copy-start.4 = (bf16[6,6,128,128]{3,2,1,0:T(8,128)(2,1)S(1)}, bf16[6,6,128,128]{3,2,1,0:T(8,128)(2,1)}, u32[]{:S(2)}) copy-start(bf16[6,6,128,128]{3,2,1,0:T(8,128)(2,1)} %fusion.7.coef_ref) | copy-start | bytes 3538948
  128.8 5.2 %copy-start.8 = (bf16[256,64]{1,0:T(8,128)(2,1)S(1)}, bf16[256,64]{1,0:T(8,128)(2,1)}, u32[]{:S(2)}) copy-start(bf16[256,64]{1,0:T(8,128)(2,1)} %dynamic-slice_maximum_fusion.phase_ref) | copy-start | bytes 98308
  128.8 5.2 %copy-start.11 = (f32[48,1]{1,0:T(8,128)S(1)}, f32[48,1]{1,0:T(8,128)}, u32[]{:S(2)}) copy-start(f32[48,1]{1,0:T(8,128)} %copy.63.counts_ref) | copy-start | bytes 580
  129.8 22.5 %all-to-all-start.2 = ((bf16[8,1,2,24,768]{4,3,2,1,0:T(8,128)(2,1)}), bf16[8,1,2,24,768]{4,3,2,1,0:T(8,128)(2,1)}, u32[]{:S(2)}, u32[]{:S(2)}) async-start(bf16[8,1,2,24,768]{4,3,2,1,0:T(8,128)(2,1)} %copy.65), calls=%async_computation.2 | async-start | bytes 1179648 | tf_op jit(solution)/shard_map/all_to_all | solution.py:336
  134.1 2.3 %copy-start.14 = (bf16[48,64,768]{2,1,0:T(8,128)(2,1)S(1)}, bf16[48,64,768]{2,1,0:T(8,128)(2,1)}, u32[]{:S(2)}) copy-start(bf16[48,64,768]{2,1,0:T(8,128)(2,1)} %copy-done.13) | copy-start | bytes 14155780
  152.3 21.0 %all-to-all-start.4 = ((bf16[8,1,2,24,768]{4,3,2,1,0:T(8,128)(2,1)}), bf16[8,1,2,24,768]{4,3,2,1,0:T(8,128)(2,1)S(1)}, u32[]{:S(2)}, u32[]{:S(2)}) async-start(bf16[8,1,2,24,768]{4,3,2,1,0:T(8,128)(2,1)} %copy.70), calls=%async_computation.4 | async-start | bytes 1179648 | tf_op jit(solution)/shard_map/all_to_all | solution.py:336

commit v3 on v2

--- a/solution.py
+++ b/solution.py
@@ -180,13 +180,37 @@
     lax.fori_loop(0, zone // 16, chunk, 0)
 
 
-def unfold_kernel(select_ref, green_ref, coef_ref, phase_ref, out_ref, half, full):
+def fill_coef(code_ref, coef_ref):
+    atoms = coef_ref.shape[3]
+    for o in range(ORB):
+        code = code_ref[:, o * atoms : (o + 1) * atoms].astype(jnp.float32)
+        sign = jnp.where(code < 0, -1.0, 1.0)
+        for p in range(ORB):
+            coef_ref[o, p] = jnp.where(jnp.abs(code) == p + 1.0, sign, 0.0).astype(jnp.bfloat16)
+
+
+def row_select(code, count):
+    place = lax.broadcasted_iota(jnp.int32, (count, code.shape[1]), 0).astype(jnp.float32) + 1.0
+    sign = jnp.where(code < 0, -1.0, 1.0)
+    return jnp.where(place == jnp.abs(code), sign, 0.0).astype(jnp.bfloat16)
+
+
+def unfold_kernel(rows_ref, green_ref, code_ref, phase_ref, out_ref, coef_ref, half, full):
     zone = phase_ref.shape[1] // 2
     basis = out_ref.shape[2]
     atoms = basis // ORB
-    half[...] = jnp.dot(select_ref[0], green_ref[0], preferred_element_type=jnp.float32).astype(
-        jnp.bfloat16
-    )
+    count = green_ref.shape[1]
+
+    @pl.when(pl.program_id(0) == 0)
+    def _():
+        fill_coef(code_ref, coef_ref)
+
+    select = jnp.concatenate(
+        [row_select(rows_ref[0, oa : oa + 1, :], count) for oa in range(ORB)], axis=1
+    )
+    half[...] = lax.dot_general(
+        select, green_ref[0], (((0,), (0,)), ((), ())), preferred_element_type=jnp.float32
+    ).astype(jnp.bfloat16)
 
     def read(oa, c, p, step):
         at = pl.ds(pl.multiple_of(oa * zone + step * 16, 16), 16)
@@ -202,11 +226,19 @@
         out_ref[oa] = (sums * (1.0 / zone)).astype(jnp.bfloat16)
 
 
-def fold_kernel(select_ref, counts_ref, green_ref, w_ref, coef_ref, phase_ref, out_ref, full, half):
+def fold_kernel(
+    rows_ref, target_ref, green_ref, w_ref, code_ref, phase_ref, out_ref, coef_ref, full, half
+):
     near = phase_ref.shape[1]
     zone = phase_ref.shape[0] // 2
     basis = green_ref.shape[2]
     atoms = basis // ORB
+    count = out_ref.shape[1]
+
+    @pl.when(pl.program_id(0) == 0)
+    def _():
+        fill_coef(code_ref, coef_ref)
+
     for oa in range(ORB):
         w = w_ref[:, oa].reshape(near, basis)
         sigma = (-(green_ref[oa].astype(jnp.float32) * w.astype(jnp.float32))).astype(jnp.bfloat16)
@@ -223,8 +255,13 @@
         half[at, c * basis + o * atoms : c * basis + (o + 1) * atoms] = value
 
     turn_columns(coef_ref, read, write, zone, atoms, True)
-    sums = jnp.dot(select_ref[0], half[...], preferred_element_type=jnp.float32)
-    out_ref[0] = (sums / counts_ref[...]).astype(jnp.bfloat16)
+    select = jnp.concatenate(
+        [row_select(rows_ref[0, oa : oa + 1, :], count) for oa in range(ORB)], axis=1
+    )
+    sums = jnp.dot(select, half[...], preferred_element_type=jnp.float32)
+    point = lax.broadcasted_iota(jnp.int32, (count, zone), 0) // ORB
+    named = jnp.where(point == target_ref[...], 1.0, 0.0)
+    out_ref[0] = (sums / jnp.sum(named, axis=1, keepdims=True)).astype(jnp.bfloat16)
 
 
 PIECES = 2
@@ -245,7 +282,6 @@
     group = sites // PIECES
     near = screened.shape[0]
     here = near * width
-    targets = kmap[:, 0]
     order = column_order(basis)
 
     sent = prepare(screened, order, width, PIECES)
@@ -266,25 +302,17 @@
     forth = lax.dynamic_slice_in_dim(forth, first_r, here, 0)
     back_t = jnp.concatenate([cos_t, -sin_t], axis=0)
     back_t = lax.dynamic_slice_in_dim(back_t, first_r, here, 1)
-    source, signs = decode(rotation)
-    orbital = jnp.arange(ORB, dtype=jnp.int32)
-    place = source - (jnp.arange(basis, dtype=jnp.int32) // ORB * ORB)[None, :]
-    place = place.reshape(zone, atoms, ORB).transpose(2, 0, 1)
-    sign = signs.reshape(zone, atoms, ORB).transpose(2, 0, 1)
-    coef = (place[:, None] == orbital[None, :, None, None]).astype(jnp.bfloat16) * sign[:, None]
-
-    first = lax.axis_index("ba") * rows // ORB + lax.axis_index("kl") * sites
-    row_place = lax.dynamic_slice_in_dim(place, first, sites, 2).transpose(2, 0, 1)
-    row_sign = lax.dynamic_slice_in_dim(sign, first, sites, 2).transpose(2, 0, 1)
-    code = targets[None, None, :] * ORB + row_place
-    hit = jnp.arange(wedges * ORB, dtype=jnp.int32)
-    code = code.reshape(sites, ORB * zone)
-    row_sign = row_sign.reshape(sites, ORB * zone)
-    select = (code[:, :, None] == hit[None, None, :]).astype(jnp.bfloat16) * row_sign[:, :, None]
-    back = (code[:, None, :] == hit[None, :, None]).astype(jnp.bfloat16) * row_sign[:, None, :]
-    counts = jnp.sum(
-        (targets[None, :] == (hit // ORB)[:, None]).astype(jnp.float32), axis=1, keepdims=True
-    )
+
+    source = jnp.where(rotation >= 0, rotation, -1 - rotation)
+    place = source - (jnp.arange(basis, dtype=jnp.int32) // ORB * ORB)[None, :] + 1
+    code = jnp.where(rotation >= 0, place, -place).astype(jnp.bfloat16)
+    code = jnp.dot(code, order, preferred_element_type=jnp.float32).astype(jnp.bfloat16)
+    first = lax.axis_index("ba") * rows + lax.axis_index("kl") * part
+    row_place = lax.dynamic_slice_in_dim(place, first, part, 1) + kmap * ORB
+    row_turn = lax.dynamic_slice_in_dim(rotation, first, part, 1)
+    row_code = jnp.where(row_turn >= 0, row_place, -row_place).astype(jnp.float32)
+    row_code = row_code.T.reshape(sites, ORB, zone)
+    targets = kmap.reshape(1, zone)
 
     whole = lambda shape: pl.BlockSpec(shape, lambda i: (0,) * len(shape))
     params = pltpu.CompilerParams(vmem_limit_bytes=40 << 20)
@@ -293,20 +321,21 @@
         unfold_kernel,
         grid=(sites,),
         in_specs=[
-            pl.BlockSpec((1, ORB * zone, wedges * ORB), lambda i: (i, 0, 0)),
+            pl.BlockSpec((1, ORB, zone), lambda i: (i, 0, 0)),
             pl.BlockSpec((1, wedges * ORB, 2 * basis), lambda i: (i, 0, 0)),
-            whole(coef.shape),
+            whole(code.shape),
             whole(forth.shape),
         ],
         out_specs=pl.BlockSpec((ORB, here, basis), lambda i: (i, 0, 0)),
         out_shape=jax.ShapeDtypeStruct((part, here, basis), jnp.bfloat16),
         scratch_shapes=[
+            pltpu.VMEM((ORB, ORB, zone, atoms), jnp.bfloat16),
             pltpu.VMEM((ORB * zone, 2 * basis), jnp.bfloat16),
             pltpu.VMEM((ORB, 2 * zone, basis), jnp.bfloat16),
         ],
         compiler_params=params,
         cost_estimate=cost,
-    )(select, green, coef, forth)
+    )(row_code, green, code, forth)
 
     outs = []
     for piece in range(PIECES):
@@ -315,22 +344,23 @@
             fold_kernel,
             grid=(group,),
             in_specs=[
-                pl.BlockSpec((1, wedges * ORB, ORB * zone), lambda i, s=skip: (i + s, 0, 0)),
-                whole((wedges * ORB, 1)),
+                pl.BlockSpec((1, ORB, zone), lambda i, s=skip: (i + s, 0, 0)),
+                whole((1, zone)),
                 pl.BlockSpec((ORB, here, basis), lambda i, s=skip: (i + s, 0, 0)),
                 pl.BlockSpec((width, ORB, near, basis), lambda i: (0, i, 0, 0)),
-                whole(coef.shape),
+                whole(code.shape),
                 whole(back_t.shape),
             ],
             out_specs=pl.BlockSpec((1, wedges * ORB, 2 * basis), lambda i: (i, 0, 0)),
             out_shape=jax.ShapeDtypeStruct((group, wedges * ORB, 2 * basis), jnp.bfloat16),
             scratch_shapes=[
+            pltpu.VMEM((ORB, ORB, zone, atoms), jnp.bfloat16),
                 pltpu.VMEM((ORB, 2 * zone, basis), jnp.bfloat16),
                 pltpu.VMEM((ORB * zone, 2 * basis), jnp.bfloat16),
             ],
             compiler_params=params,
             cost_estimate=cost,
-        )(back, counts, green_r, w[piece], coef, back_t)
+        )(row_code, targets, green_r, w[piece], code, back_t)
         folded = folded.reshape(group, wedges, ORB, 2, basis).transpose(1, 3, 0, 2, 4)
         folded = folded.reshape(width * halves, own, 2, each, basis)
         folded = lax.all_to_all(folded, both, split_axis=0, concat_axis=0, tiled=True)

time: 178 us -> 172 us (0.966)
  waiting for transfers between devices: 30.5 us -> 48.4 us
  local copies, waits for them, and re-layouts: 40.2 us -> 23.5 us
  other arithmetic: 13.4 us -> 3.22 us
    all_to_all x2, waiting for transfers between devices: 0.01 us -> 16.5 us  [per_device_rows(): lax.all_to_all(x, 'kl', split_axis=0, concat_axis=0, tiled=True)]
    mul x5 -> x1, other arithmetic: 7 us -> 0.01 us  [per_device_rows(): jnp.arange(basis, dtype=jnp.int32) // ORB * ORB]
    unnamed x45 -> x36, local copies, waits for them, and re-layouts: 17.3 us -> 13.3 us
    transpose x2 -> x1, local copies, waits for them, and re-layouts: 2.79 us -> 0.06 us  [per_device_rows(): row_code = row_code.T.reshape(sites, ORB, zone)]
    reshape x2 -> x1, local copies, waits for them, and re-layouts: 2.75 us -> 0.02 us  [per_device_rows(): row_code = row_code.T.reshape(sites, ORB, zone)]
    sub x1 -> x0, local copies, waits for them, and re-layouts: 1.92 us -> none  [per_device_rows(): place = source - (jnp.arange(basis, dtype=jnp.int32) // ORB * ORB)[None, :]]
    reshape x4, local copies, waits for them, and re-layouts: 2.22 us -> 0.39 us  [per_device_rows(): folded.reshape(group, wedges, ORB, 2, basis).transpose(1, 3, 0, 2, 4)]
  transfers between devices with their start and end apart: 5 -> 5, of which waited for: 2 -> 3; matrix products, arithmetic and copies ran while one was open for 20% -> 7% of each run, Pallas kernels for 36% -> 37%
where the time goes in v3:
time: 172 us; the launch traced here: 171 us
  Pallas kernels  63.6 us (37%)
  waiting for transfers between devices  48.4 us (28%)
  starting transfers between devices  26.6 us (15%)
  local copies, waits for them, and re-layouts  23.5 us (14%)
  matrix products  5.33 us (3%)
  other arithmetic  3.22 us (2%)
    pallas_call x2, Pallas kernels, per_device_rows(): pl.pallas_call(fold_kernel, grid=(group,), in_specs=[pl.BlockSpec((1, ORB...  29.1 us
    pallas_call x1, Pallas kernels, per_device_rows(): pl.pallas_call(unfold_kernel, grid=(sites,), in_specs=[pl.BlockSpec((1, O...  27.8 us
    all_to_all x1, waiting for transfers between devices, per_device_rows(): green = lax.all_to_all(green, both, split_axis=0, concat_axis=0, tiled=True)  17.7 us
    all_to_all x2, waiting for transfers between devices, per_device_rows(): lax.all_to_all(x, 'kl', split_axis=0, concat_axis=0, tiled=True)  16.5 us
    all_to_all x2, waiting for transfers between devices, per_device_rows(): lax.all_to_all(folded, both, split_axis=0, concat_axis=0, tiled=True)  14.2 us
    unnamed x36, local copies, waits for them, and re-layouts  13.3 us
    all_to_all x2, starting transfers between devices, per_device_rows(): lax.all_to_all(folded, both, split_axis=0, concat_axis=0, tiled=True)  11.2 us
    all_to_all x2, starting transfers between devices, per_device_rows(): lax.all_to_all(x, 'kl', split_axis=0, concat_axis=0, tiled=True)  8.13 us
  transfers between devices with their start and end apart: 5, of which 3 were waited for; matrix products, arithmetic and copies ran while one was open for 7% of the time, Pallas kernels for 37%

profile of v3, /device:TPU:0, one launch (start us, length us, event | category | flops | bytes accessed | tf_op | source)
XLA Modules:
  0.0 171.0 jit_solution(4958158728637681650)
XLA Ops:
  0.0 0.0 copy-start
  0.0 1.1 copy-done
  1.1 0.8 fusion.7
  1.9 1.1 pad_maximum_fusion
  3.1 7.3 %all-to-all-start = ((bf16[8,1,2,48,768]{4,3,2,1,0:T(8,128)(2,1)}), bf16[8,1,2,48,768]{4,3,2,1,0:T(8,128)(2,1)S(1)}, u32[]{:S(2)}, u32[]{:S(2)}) async-start(bf16[8,1,2,48,768]{4,3,2,1,0:T(8,128)(2,1)} %pad_maximum_fusion), calls=%async_computation | async-start | bytes 2359296 | tf_op jit(solution)/shard_map/all_to_all | solution.py:295
  10.3 0.1 fusion.20.swap_ref
  10.5 0.3 fusion.4.order_ref
  10.7 0.0 copy-start.8
  10.7 2.3 %copy-done.8 = bf16[16,192,768]{2,1,0:T(8,128)(2,1)S(1)} copy-done((bf16[16,192,768]{2,1,0:T(8,128)(2,1)S(1)}, bf16[16,192,768]{2,1,0:T(8,128)(2,1)}, u32[]{:S(2)}) %copy-start.8) | copy-done | bytes 4718616
  13.1 6.7 %shard_map.47 = (bf16[4,24,16,768]{3,2,1,0:T(8,128)(2,1)}, bf16[4,24,16,768]{3,2,1,0:T(8,128)(2,1)S(1)}) custom-call(bf16[256,256]{1,0:T(8,128)(2,1)S(1)} %fusion.20.swap_ref, bf16[768,768]{1,0:T(8,128)(2,1)S(1)} %fusion.4.order_ref, bf16[16,192,768]{2,1,0:T(8,128)(2,1)S(1)} %copy-done.8), custom_call_target="tpu_custom_call" | custom-call | flops 4800000000 | bytes 9437184 | tf_op jit(solution)/shard_map/pallas_call | solution.py:148
  19.8 1.4 copy-done.1
  21.2 17.7 %all-to-all-done = bf16[8,1,2,48,768]{4,3,2,1,0:T(8,128)(2,1)S(1)} async-done(((bf16[8,1,2,48,768]{4,3,2,1,0:T(8,128)(2,1)}), bf16[8,1,2,48,768]{4,3,2,1,0:T(8,128)(2,1)S(1)}, u32[]{:S(2)}, u32[]{:S(2)}) %all-to-all-start) | async-done | bytes 1179680 | tf_op jit(solution)/shard_map/all_to_all | solution.py:295
  38.9 1.0 copy-done.15
  39.9 3.6 %all-to-all-start.3 = ((bf16[4,24,16,768]{3,2,1,0:T(8,128)(2,1)}), bf16[4,24,16,768]{3,2,1,0:T(8,128)(2,1)S(1)}, u32[]{:S(2)}, u32[]{:S(2)}) async-start(bf16[4,24,16,768]{3,2,1,0:T(8,128)(2,1)} %copy-done.1), calls=%async_computation.3 | async-start | bytes 4718592 | tf_op jit(solution)/shard_map/all_to_all | solution.py:288
  43.6 0.0 copy-done.9
  43.6 0.0 copy-done.17
  43.6 0.1 fusion.18
  43.7 0.1 fusion.25
  43.8 0.1 copy.23
  43.9 0.0 copy-start.5
  43.9 0.0 copy-start.16
  44.0 0.4 fusion.29
  44.3 0.4 cosine_convert_fusion
  44.7 0.7 dynamic-slice_maximum_fusion.phase_ref
  45.4 1.7 %fusion.16.code_ref = bf16[128,768]{1,0:T(8,128)(2,1)S(1)} fusion(s32[768]{0:T(1024)S(1)} %fusion.38, s32[128,768]{1,0:T(8,128)} %param.7, s32[768]{0:T(1024)S(1)} %broadcast_multiply_fusion), kind=kOutput, calls=%fused_computation.19 | convolution fusion | flops 152469504 | bytes 595968 | tf_op jit(solution)/shard_map/dot_general | solution.py:309
  47.1 0.0 copy-done.16
  47.1 0.0 copy-start.10
  47.2 0.7 copy.25
  47.8 2.2 %copy.26 = bf16[8,8,6,2,768]{4,3,2,1,0:T(2,128)(2,1)} copy(bf16[8,8,6,2,768]{4,1,2,0,3:T(8,128)(2,1)S(1)} %bitcast.42) | data formatting | bytes 2359296 | tf_op jit(solution)/shard_map/transpose | solution.py:296
  50.0 3.8 %reshape.193.green_ref = bf16[8,48,1536]{2,1,0:T(8,128)(2,1)} reshape(bf16[8,8,6,2,768]{4,3,2,1,0:T(2,128)(2,1)} %copy.26) | data formatting | bytes 2359296 | tf_op jit(solution)/shard_map/reshape | solution.py:297
  53.9 16.5 %all-to-all-done.3.w_ref = bf16[4,24,16,768]{3,2,1,0:T(8,128)(2,1)S(1)} async-done(((bf16[4,24,16,768]{3,2,1,0:T(8,128)(2,1)}), bf16[4,24,16,768]{3,2,1,0:T(8,128)(2,1)S(1)}, u32[]{:S(2)}, u32[]{:S(2)}) %all-to-all-start.3) | async-done | bytes 2359328 | tf_op jit(solution)/shard_map/all_to_all | solution.py:288
  70.4 4.5 %all-to-all-start.1 = ((bf16[4,24,16,768]{3,2,1,0:T(8,128)(2,1)}), bf16[4,24,16,768]{3,2,1,0:T(8,128)(2,1)}, u32[]{:S(2)}, u32[]{:S(2)}) async-start(bf16[4,24,16,768]{3,2,1,0:T(8,128)(2,1)} %get-tuple-element.7), calls=%async_computation.1 | async-start | bytes 4718592 | tf_op jit(solution)/shard_map/all_to_all | solution.py:288
  74.9 0.0 copy-done.5
  74.9 0.0 copy-done.10
  74.9 0.0 copy-start.2
  74.9 1.3 copy-done.2
  76.2 27.8 %shard_map.46.green_ref = bf16[48,64,768]{2,1,0:T(8,128)(2,1)S(1)} custom-call(f32[8,6,128]{2,1,0:T(8,128)S(1)} %reshape.188.rows_ref, bf16[8,48,1536]{2,1,0:T(8,128)(2,1)S(1)} %copy-done.2, bf16[128,768]{1,0:T(8,128)(2,1)S(1)} %fusion.16.code_ref, bf16[64,256]{1,0:T(8,128)(2,1)S(1)} %fusion.30.phase_ref), custom_call_target="tpu_custom_call" | custom-call | flops 20000000000 | bytes 12582912 | tf_op jit(solution)/shard_map/pallas_call | solution.py:320
  103.9 0.0 copy-done.3
  103.9 0.0 copy-start.6
  103.9 0.7 copy-done.6
  104.7 0.9 copy-done.11
  105.6 14.1 %shard_map.49 = bf16[4,48,1536]{2,1,0:T(8,128)(2,1)S(1)} custom-call(f32[8,6,128]{2,1,0:T(8,128)S(1)} %copy-done.6, s32[1,128]{1,0:T(1,128)S(1)} %bitcast.40, bf16[48,64,768]{2,1,0:T(8,128)(2,1)S(1)} %shard_map.46.green_ref, bf16[4,24,16,768]{3,2,1,0:T(8,128)(2,1)S(1)} %all-to-all-done.3.w_ref, bf16[128,768]{1,0:T(8,128)(2,1)S(1)} %copy-done.11, ...), custom_call_target="tpu_custom_call" | custom-call | flops 20000000000 | bytes 12582912 | tf_op jit(solution)/shard_map/pallas_call | solution.py:343
  119.7 0.0 copy-start.13
  119.7 2.1 %copy-done.13 = bf16[48,64,768]{2,1,0:T(8,128)(2,1)} copy-done((bf16[48,64,768]{2,1,0:T(8,128)(2,1)}, bf16[48,64,768]{2,1,0:T(8,128)(2,1)S(1)}, u32[]{:S(2)}) %copy-start.13) | copy-done | bytes 4718616
  121.9 0.1 reshape.196
  122.0 0.1 copy.31
  122.1 0.9 copy.32
  123.0 0.0 all-to-all-done.1.w_ref
  123.0 5.2 %all-to-all-start.4 = ((bf16[8,1,2,24,768]{4,3,2,1,0:T(8,128)(2,1)}), bf16[8,1,2,24,768]{4,3,2,1,0:T(8,128)(2,1)S(1)}, u32[]{:S(2)}, u32[]{:S(2)}) async-start(bf16[8,1,2,24,768]{4,3,2,1,0:T(8,128)(2,1)} %copy.32), calls=%async_computation.4 | async-start | bytes 1179648 | tf_op jit(solution)/shard_map/all_to_all | solution.py:366
  128.2 0.0 copy-done.4
  128.3 2.3 %copy-done.14 = bf16[48,64,768]{2,1,0:T(8,128)(2,1)S(1)} copy-done((bf16[48,64,768]{2,1,0:T(8,128)(2,1)S(1)}, bf16[48,64,768]{2,1,0:T(8,128)(2,1)}, u32[]{:S(2)}) %copy-start.14) | copy-done | bytes 4718616
  130.6 15.0 %shard_map.48 = bf16[4,48,1536]{2,1,0:T(8,128)(2,1)S(1)} custom-call(f32[8,6,128]{2,1,0:T(8,128)S(1)} %copy-done.7, s32[1,128]{1,0:T(1,128)S(1)} %bitcast.41, bf16[48,64,768]{2,1,0:T(8,128)(2,1)S(1)} %copy-done.14, bf16[4,24,16,768]{3,2,1,0:T(8,128)(2,1)} %all-to-all-done.1.w_ref, bf16[128,768]{1,0:T(8,128)(2,1)S(1)} %copy-done.12, bf16[256,64]{1,0:T(8,128)(2,1)S(1)} %copy-done.4), custom_call_target="tpu_custom_call" | custom-call | flops 20000000000 | bytes 12582912 | tf_op jit(solution)/shard_map/pallas_call | solution.py:343
  145.6 0.1 reshape.194
  145.7 0.1 copy.27
  145.8 0.9 copy.28
  146.7 0.0 all-to-all-done.4
  146.7 6.0 %all-to-all-start.2 = ((bf16[8,1,2,24,768]{4,3,2,1,0:T(8,128)(2,1)}), bf16[8,1,2,24,768]{4,3,2,1,0:T(8,128)(2,1)S(1)}, u32[]{:S(2)}, u32[]{:S(2)}) async-start(bf16[8,1,2,24,768]{4,3,2,1,0:T(8,128)(2,1)} %copy.28), calls=%async_computation.2 | async-start | bytes 1179648 | tf_op jit(solution)/shard_map/all_to_all | solution.py:366
  152.8 14.2 %all-to-all-done.2 = bf16[8,1,2,24,768]{4,3,2,1,0:T(8,128)(2,1)S(1)} async-done(((bf16[8,1,2,24,768]{4,3,2,1,0:T(8,128)(2,1)}), bf16[8,1,2,24,768]{4,3,2,1,0:T(8,128)(2,1)S(1)}, u32[]{:S(2)}, u32[]{:S(2)}) %all-to-all-start.2) | async-done | bytes 589856 | tf_op jit(solution)/shard_map/all_to_all | solution.py:366
  167.0 0.7 fusion.2
  167.7 0.7 fusion
  168.4 0.7 fusion.8
  169.1 0.7 fusion.9
  169.8 0.1 maximum_bitcast_fusion
  169.9 1.1 copy.35
  (23 shorter events, 0.2 us)
Async XLA Ops:
  0.0 1.1 copy-start
  3.1 35.9 %all-to-all-start = ((bf16[8,1,2,48,768]{4,3,2,1,0:T(8,128)(2,1)}), bf16[8,1,2,48,768]{4,3,2,1,0:T(8,128)(2,1)S(1)}, u32[]{:S(2)}, u32[]{:S(2)}) async-start(bf16[8,1,2,48,768]{4,3,2,1,0:T(8,128)(2,1)} %pad_maximum_fusion), calls=%async_computation | async-start | bytes 2359296 | tf_op jit(solution)/shard_map/all_to_all | solution.py:295
  10.7 2.3 %copy-start.8 = (bf16[16,192,768]{2,1,0:T(8,128)(2,1)S(1)}, bf16[16,192,768]{2,1,0:T(8,128)(2,1)}, u32[]{:S(2)}) copy-start(bf16[16,192,768]{2,1,0:T(8,128)(2,1)} %w_ref.1) | copy-start | bytes 14155780
  19.8 1.4 copy-start.1
  38.9 1.0 copy-start.15
  38.9 4.7 %copy-start.9 = (s32[128,1]{0,1:T(1,128)S(1)}, s32[128,1]{0,1:T(1,128)}, u32[]{:S(2)}) copy-start(s32[128,1]{0,1:T(1,128)} %param.6) | copy-start | bytes 1540
  38.9 4.7 %copy-start.17 = (s32[128,768]{1,0:T(8,128)S(1)}, s32[128,768]{1,0:T(8,128)}, u32[]{:S(2)}) copy-start(s32[128,768]{1,0:T(8,128)} %param.7) | copy-start | bytes 1179652
  39.9 30.4 %all-to-all-start.3 = ((bf16[4,24,16,768]{3,2,1,0:T(8,128)(2,1)}), bf16[4,24,16,768]{3,2,1,0:T(8,128)(2,1)S(1)}, u32[]{:S(2)}, u32[]{:S(2)}) async-start(bf16[4,24,16,768]{3,2,1,0:T(8,128)(2,1)} %copy-done.1), calls=%async_computation.3 | async-start | bytes 4718592 | tf_op jit(solution)/shard_map/all_to_all | solution.py:288
  43.9 30.9 %copy-start.5 = (f32[8,6,128]{2,1,0:T(8,128)}, f32[8,6,128]{2,1,0:T(8,128)S(1)}, u32[]{:S(2)}) copy-start(f32[8,6,128]{2,1,0:T(8,128)S(1)} %reshape.188.rows_ref) | copy-start | bytes 73732
  43.9 3.2 %copy-start.16 = (bf16[8,1,2,48,768]{4,3,2,1,0:T(8,128)(2,1)S(1)}, bf16[8,1,2,48,768]{4,3,2,1,0:T(8,128)(2,1)}, u32[]{:S(2)}) copy-start(bf16[8,1,2,48,768]{4,3,2,1,0:T(8,128)(2,1)} %copy-done.15) | copy-start | bytes 3538948
  47.1 27.7 %copy-start.10 = (bf16[128,768]{1,0:T(8,128)(2,1)}, bf16[128,768]{1,0:T(8,128)(2,1)S(1)}, u32[]{:S(2)}) copy-start(bf16[128,768]{1,0:T(8,128)(2,1)S(1)} %fusion.16.code_ref) | copy-start | bytes 589828
  70.4 52.7 %all-to-all-start.1 = ((bf16[4,24,16,768]{3,2,1,0:T(8,128)(2,1)}), bf16[4,24,16,768]{3,2,1,0:T(8,128)(2,1)}, u32[]{:S(2)}, u32[]{:S(2)}) async-start(bf16[4,24,16,768]{3,2,1,0:T(8,128)(2,1)} %get-tuple-element.7), calls=%async_computation.1 | async-start | bytes 4718592 | tf_op jit(solution)/shard_map/all_to_all | solution.py:288
  74.9 1.3 copy-start.2
  76.2 27.8 %copy-start.3 = (bf16[256,64]{1,0:T(8,128)(2,1)S(1)}, bf16[256,64]{1,0:T(8,128)(2,1)}, u32[]{:S(2)}) copy-start(bf16[256,64]{1,0:T(8,128)(2,1)} %dynamic-slice_maximum_fusion.phase_ref) | copy-start | bytes 98308
  103.9 0.8 copy-start.6
  104.7 0.9 copy-start.11
  119.7 2.2 %copy-start.13 = (bf16[48,64,768]{2,1,0:T(8,128)(2,1)}, bf16[48,64,768]{2,1,0:T(8,128)(2,1)S(1)}, u32[]{:S(2)}) copy-start(bf16[48,64,768]{2,1,0:T(8,128)(2,1)S(1)} %shard_map.46.green_ref) | copy-start | bytes 14155780
  121.9 6.3 %copy-start.4 = (bf16[256,64]{1,0:T(8,128)(2,1)S(1)}, bf16[256,64]{1,0:T(8,128)(2,1)}, u32[]{:S(2)}) copy-start(bf16[256,64]{1,0:T(8,128)(2,1)} %dynamic-slice_maximum_fusion.phase_ref) | copy-start | bytes 98308
  121.9 6.4 %copy-start.7 = (f32[8,6,128]{2,1,0:T(8,128)S(1)}, f32[8,6,128]{2,1,0:T(8,128)}, u32[]{:S(2)}) copy-start(f32[8,6,128]{2,1,0:T(8,128)} %copy-done.5) | copy-start | bytes 73732
  121.9 6.4 %copy-start.12 = (bf16[128,768]{1,0:T(8,128)(2,1)S(1)}, bf16[128,768]{1,0:T(8,128)(2,1)}, u32[]{:S(2)}) copy-start(bf16[128,768]{1,0:T(8,128)(2,1)} %copy-done.10) | copy-start | bytes 589828
  123.0 23.7 %all-to-all-start.4 = ((bf16[8,1,2,24,768]{4,3,2,1,0:T(8,128)(2,1)}), bf16[8,1,2,24,768]{4,3,2,1,0:T(8,128)(2,1)S(1)}, u32[]{:S(2)}, u32[]{:S(2)}) async-start(bf16[8,1,2,24,768]{4,3,2,1,0:T(8,128)(2,1)} %copy.32), calls=%async_computation.4 | async-start | bytes 1179648 | tf_op jit(solution)/shard_map/all_to_all | solution.py:366
  128.2 2.3 %copy-start.14 = (bf16[48,64,768]{2,1,0:T(8,128)(2,1)S(1)}, bf16[48,64,768]{2,1,0:T(8,128)(2,1)}, u32[]{:S(2)}) copy-start(bf16[48,64,768]{2,1,0:T(8,128)(2,1)} %copy-done.13) | copy-start | bytes 14155780
  146.7 20.2 %all-to-all-start.2 = ((bf16[8,1,2,24,768]{4,3,2,1,0:T(8,128)(2,1)}), bf16[8,1,2,24,768]{4,3,2,1,0:T(8,128)(2,1)S(1)}, u32[]{:S(2)}, u32[]{:S(2)}) async-start(bf16[8,1,2,24,768]{4,3,2,1,0:T(8,128)(2,1)} %copy.28), calls=%async_computation.2 | async-start | bytes 1179648 | tf_op jit(solution)/shard_map/all_to_all | solution.py:366

commit v4 on v0

--- a/solution.py
+++ b/solution.py
@@ -1,8 +1,12 @@
+import functools
 import math
 
 import jax
 import jax.numpy as jnp
 from jax import lax
+from jax.experimental import pallas as pl
+from jax.experimental.pallas import tpu as pltpu
+from jax.sharding import Mesh
 from jax.sharding import PartitionSpec as P
 
 KX = 8
@@ -51,7 +55,7 @@
     )
 
 
-def per_device(green_irr, screened, kmap, rotation):
+def per_device_columns(green_irr, screened, kmap, rotation):
     width_ka = lax.axis_size("ka")
     place_ka = lax.axis_index("ka")
     place_ba = lax.axis_index("ba")
@@ -110,8 +114,377 @@
     ).astype(folded.dtype)
 
 
+ORB = 6
+
+
+def column_order(basis):
+    atoms = basis // ORB
+    place = jnp.arange(basis, dtype=jnp.int32)
+    moved = (place % ORB) * atoms + place // ORB
+    return (moved[:, None] == place[None, :]).astype(jnp.bfloat16)
+
+
+def turn_columns(coef_ref, parts, src, dst, zone, back):
+    def chunk(step, carry):
+        at = pl.ds(pl.multiple_of(step * 16, 16), 16)
+        coef = [[coef_ref[o, p, at, :] for p in range(ORB)] for o in range(ORB)]
+        for oa in range(ORB):
+            for c in parts:
+                given = [src(oa, c, p, step) for p in range(ORB)]
+                for o in range(ORB):
+                    total = None
+                    for p in range(ORB):
+                        term = (coef[p][o] if back else coef[o][p]) * given[p]
+                        total = term if total is None else total + term
+                    dst(oa, c, o, step, total)
+        return carry
+
+    lax.fori_loop(0, zone // 16, chunk, 0)
+
+
+def fill_coef(code_ref, coef_ref):
+    atoms = coef_ref.shape[3]
+    for o in range(ORB):
+        code = code_ref[:, o * atoms : (o + 1) * atoms].astype(jnp.float32)
+        sign = jnp.where(code < 0, -1.0, 1.0)
+        for p in range(ORB):
+            coef_ref[o, p] = jnp.where(jnp.abs(code) == p + 1.0, sign, 0.0).astype(jnp.bfloat16)
+
+
+def row_select(code, count):
+    place = lax.broadcasted_iota(jnp.int32, (count, code.shape[1]), 0).astype(jnp.float32) + 1.0
+    sign = jnp.where(code < 0, -1.0, 1.0)
+    return jnp.where(place == jnp.abs(code), sign, 0.0).astype(jnp.bfloat16)
+
+
+def site_select(rows_ref, site, count):
+    return jnp.concatenate(
+        [row_select(rows_ref[site, oa : oa + 1, :], count) for oa in range(ORB)], axis=1
+    )
+
+
+def kernel(
+    halves, width, swap_ref, order_ref, site_ref, green_ref, w_ref, rows_ref, target_ref,
+    code_ref, forth_ref, back_ref, out_ref,
+    g_send, g_recv, g_all, w_send, w_recv, green_r, coef_ref, half, full, stage, o_send, o_recv,
+    g_out, g_in, w_out, w_in, o_out, o_in,
+):
+    total = halves * width
+    kh, kl = lax.axis_index("kh"), lax.axis_index("kl")
+    me = kh * width + kl
+    near, rows, basis = w_ref.shape
+    zone = code_ref.shape[0]
+    atoms = basis // ORB
+    part = rows // width
+    sites = part // ORB
+    count = total * ORB
+    step = swap_ref.shape[0] // near
+    here = near * width
+    f32, bf16 = jnp.float32, jnp.bfloat16
+
+    def peer(off):
+        other = lax.rem(me + off, total)
+        return other, {"kh": other // width, "kl": lax.rem(other, width)}
+
+    barrier = pltpu.get_barrier_semaphore()
+    for off in range(1, total):
+        pl.semaphore_signal(
+            barrier, inc=1, device_id=peer(off)[1], device_id_type=pl.DeviceIdType.MESH
+        )
+    pl.semaphore_wait(barrier, total - 1)
+
+    def green_copy(off):
+        other, where = peer(off)
+        return pltpu.make_async_remote_copy(
+            src_ref=g_send.at[lax.rem(other, width)],
+            dst_ref=g_recv.at[me],
+            send_sem=g_out.at[off - 1],
+            recv_sem=g_in.at[off - 1],
+            device_id=where,
+            device_id_type=pl.DeviceIdType.MESH,
+        )
+
+    for c in range(2):
+        moved = jnp.dot(
+            green_ref[c * rows : (c + 1) * rows, :], order_ref[...], preferred_element_type=f32
+        ).astype(bf16)
+        for k in range(width):
+            g_send[k, c] = moved[k * part : (k + 1) * part]
+    for off in range(1, total):
+        green_copy(off).start()
+    g_recv[me] = g_send[kl]
+
+    blocks = part // step
+
+    def w_place(t):
+        off = 1 + lax.rem(t, width - 1)
+        return lax.rem(kl + off, width), t // (width - 1)
+
+    def w_copy(t):
+        to, b = w_place(t)
+        at = pl.ds(b * step, step)
+        return pltpu.make_async_remote_copy(
+            src_ref=w_send.at[to, at],
+            dst_ref=w_recv.at[kl, at],
+            send_sem=w_out.at[t],
+            recv_sem=w_in.at[t],
+            device_id={"kh": kh, "kl": to},
+            device_id_type=pl.DeviceIdType.MESH,
+        )
+
+    def prepared(to, b):
+        at = pl.ds(pl.multiple_of(to * part + b * step, step), step)
+        block = w_ref[:, at, :].reshape(near * step, basis)
+        turned = jnp.dot(swap_ref[...], block, preferred_element_type=f32).astype(bf16)
+        out = jnp.dot(turned, order_ref[...], preferred_element_type=f32).astype(bf16)
+        return out.reshape(step, near, basis)
+
+    def w_start(t, carry):
+        to, b = w_place(t)
+        w_send[to, pl.ds(b * step, step)] = prepared(to, b)
+        w_copy(t).start()
+        return carry
+
+    lax.fori_loop(0, blocks * (width - 1), w_start, 0)
+
+    def w_own(b, carry):
+        w_recv[kl, pl.ds(b * step, step)] = prepared(kl, b)
+        return carry
+
+    lax.fori_loop(0, blocks, w_own, 0)
+    fill_coef(code_ref, coef_ref)
+
+    for off in range(1, total):
+        green_copy(off).wait_recv()
+    for c in range(2):
+        given = g_recv[:, c].reshape(total * part, basis)
+        g_all[:, :, c * basis : (c + 1) * basis] = (
+            lax.dot_general(
+                site_ref[...], given, (((0,), (0,)), ((), ())), preferred_element_type=f32
+            )
+            .astype(bf16)
+            .reshape(sites, count, basis)
+        )
+
+    def unfold(site, carry):
+        half[...] = lax.dot_general(
+            site_select(rows_ref, site, count),
+            g_all[site],
+            (((0,), (0,)), ((), ())),
+            preferred_element_type=f32,
+        ).astype(bf16)
+
+        def read(oa, c, p, at):
+            at = pl.ds(pl.multiple_of(oa * zone + at * 16, 16), 16)
+            return half[at, c * basis + p * atoms : c * basis + (p + 1) * atoms]
+
+        def write(oa, c, o, at, value):
+            at = pl.ds(pl.multiple_of(c * zone + at * 16, 16), 16)
+            full[oa, at, o * atoms : (o + 1) * atoms] = value
+
+        turn_columns(coef_ref, (0, 1), read, write, zone, False)
+        for oa in range(ORB):
+            sums = jnp.dot(forth_ref[...], full[oa], preferred_element_type=f32)
+            green_r[site * ORB + oa] = (sums * (1.0 / zone)).astype(bf16)
+        return carry
+
+    lax.fori_loop(0, sites, unfold, 0)
+
+    def w_arrived(t, carry):
+        w_copy(t).wait_recv()
+        return carry
+
+    lax.fori_loop(0, blocks * (width - 1), w_arrived, 0)
+
+    point = lax.broadcasted_iota(jnp.int32, (count, zone), 0) // ORB
+    named = jnp.where(point == target_ref[...], 1.0, 0.0)
+    counts = jnp.sum(named, axis=1, keepdims=True)
+
+    def out_copy(off, c):
+        other, where = peer(off)
+        return pltpu.make_async_remote_copy(
+            src_ref=o_send.at[other, c],
+            dst_ref=o_recv.at[me, c],
+            send_sem=o_out.at[c, off - 1],
+            recv_sem=o_in.at[c, off - 1],
+            device_id=where,
+            device_id_type=pl.DeviceIdType.MESH,
+        )
+
+    for c in range(2):
+
+        def fold(site, carry, c=c):
+            for oa in range(ORB):
+                row = site * ORB + oa
+                if c == 0:
+                    w = w_recv[:, row].reshape(here, basis).astype(f32)
+                    sigma = (-(green_r[row].astype(f32) * w)).astype(bf16)
+                    green_r[row] = sigma
+                else:
+                    sigma = green_r[row]
+                full[oa, 0:zone] = jnp.dot(
+                    back_ref[c * zone : (c + 1) * zone, :], sigma, preferred_element_type=f32
+                ).astype(bf16)
+
+            def read(oa, c, p, at):
+                at = pl.ds(pl.multiple_of(at * 16, 16), 16)
+                return full[oa, at, p * atoms : (p + 1) * atoms]
+
+            def write(oa, c, o, at, value):
+                at = pl.ds(pl.multiple_of(oa * zone + at * 16, 16), 16)
+                half[at, o * atoms : (o + 1) * atoms] = value
+
+            turn_columns(coef_ref, (c,), read, write, zone, True)
+            sums = jnp.dot(
+                site_select(rows_ref, site, count), half[:, 0:basis], preferred_element_type=f32
+            )
+            stage[site] = (sums / counts).astype(bf16)
+            return carry
+
+        lax.fori_loop(0, sites, fold, 0)
+        o_send[:, c] = (
+            jnp.dot(
+                site_ref[...], stage[...].reshape(sites * count, basis), preferred_element_type=f32
+            )
+            .astype(bf16)
+            .reshape(total, part, basis)
+        )
+        for off in range(1, total):
+            out_copy(off, c).start()
+        o_recv[me, c] = o_send[me, c]
+
+    for c in range(2):
+        for off in range(1, total):
+            out_copy(off, c).wait_recv()
+        sums = None
+        for h in range(halves):
+            given = o_recv[h * width : (h + 1) * width, c].reshape(rows, basis)
+            term = lax.dot_general(
+                given, order_ref[...], (((1,), (1,)), ((), ())), preferred_element_type=f32
+            )
+            sums = term if sums is None else sums + term
+        out_ref[c] = sums
+
+    for off in range(1, total):
+        green_copy(off).wait_send()
+        for c in range(2):
+            out_copy(off, c).wait_send()
+
+    def w_sent(t, carry):
+        w_copy(t).wait_send()
+        return carry
+
+    lax.fori_loop(0, blocks * (width - 1), w_sent, 0)
+
+
+HALVES = 2
+STEP = 16
+
+
+def per_device_rows(green_irr, screened, kmap, rotation):
+    halves = lax.axis_size("kh")
+    width = lax.axis_size("kl")
+    total = halves * width
+    zone, basis = rotation.shape
+    rows = green_irr.shape[2]
+    part = rows // width
+    sites = part // ORB
+    near = screened.shape[0]
+    here = near * width
+    count = total * ORB
+    order = column_order(basis)
+
+    place = jnp.arange(near * STEP, dtype=jnp.int32)
+    swap = ((place % near * STEP + place // near)[:, None] == place[None, :]).astype(jnp.bfloat16)
+    place = jnp.arange(total * part, dtype=jnp.int32)
+    origin = place % part // ORB * count + place // part * ORB + place % ORB
+    site = (origin[:, None] == place[None, :]).astype(jnp.bfloat16)
+
+    cos_t, sin_t = phase_tables(zone)
+    first_r = lax.axis_index("kh") * here
+    forth = jnp.concatenate([cos_t, -sin_t], axis=1)
+    forth = lax.dynamic_slice_in_dim(forth, first_r, here, 0)
+    back_t = jnp.concatenate([cos_t, -sin_t], axis=0)
+    back_t = lax.dynamic_slice_in_dim(back_t, first_r, here, 1)
+
+    source = jnp.where(rotation >= 0, rotation, -1 - rotation)
+    place = source - (jnp.arange(basis, dtype=jnp.int32) // ORB * ORB)[None, :] + 1
+    code = jnp.where(rotation >= 0, place, -place).astype(jnp.bfloat16)
+    code = jnp.dot(code, order, preferred_element_type=jnp.float32).astype(jnp.bfloat16)
+    first = lax.axis_index("ba") * rows + lax.axis_index("kl") * part
+    row_place = lax.dynamic_slice_in_dim(place, first, part, 1) + kmap * ORB
+    row_turn = lax.dynamic_slice_in_dim(rotation, first, part, 1)
+    row_code = jnp.where(row_turn >= 0, row_place, -row_place).astype(jnp.float32)
+    row_code = row_code.T.reshape(sites, ORB, zone)
+    targets = kmap.reshape(1, zone)
+
+    bf16 = jnp.bfloat16
+    vmem = pl.BlockSpec(memory_space=pltpu.VMEM)
+    copies = part // STEP * (width - 1)
+    out = pl.pallas_call(
+        functools.partial(kernel, halves, width),
+        in_specs=[vmem] * 10,
+        out_specs=vmem,
+        out_shape=jax.ShapeDtypeStruct((2, rows, basis), jnp.float32),
+        scratch_shapes=[
+            pltpu.VMEM((width, 2, part, basis), bf16),
+            pltpu.VMEM((total, 2, part, basis), bf16),
+            pltpu.VMEM((sites, count, 2 * basis), bf16),
+            pltpu.VMEM((width, part, near, basis), bf16),
+            pltpu.VMEM((width, part, near, basis), bf16),
+            pltpu.VMEM((part, here, basis), bf16),
+            pltpu.VMEM((ORB, ORB, zone, basis // ORB), bf16),
+            pltpu.VMEM((ORB * zone, 2 * basis), bf16),
+            pltpu.VMEM((ORB, 2 * zone, basis), bf16),
+            pltpu.VMEM((sites, count, basis), bf16),
+            pltpu.VMEM((total, 2, part, basis), bf16),
+            pltpu.VMEM((total, 2, part, basis), bf16),
+            pltpu.SemaphoreType.DMA((total - 1,)),
+            pltpu.SemaphoreType.DMA((total - 1,)),
+            pltpu.SemaphoreType.DMA((copies,)),
+            pltpu.SemaphoreType.DMA((copies,)),
+            pltpu.SemaphoreType.DMA((2, total - 1)),
+            pltpu.SemaphoreType.DMA((2, total - 1)),
+        ],
+        compiler_params=pltpu.CompilerParams(
+            collective_id=0, has_side_effects=True, vmem_limit_bytes=52 << 20
+        ),
+        cost_estimate=pl.CostEstimate(
+            flops=60000000000, bytes_accessed=12 << 20, transcendentals=0
+        ),
+    )(
+        swap, order, site, green_irr.reshape(2 * rows, basis), screened, row_code, targets,
+        code, forth, back_t,
+    )
+    return out.reshape(1, 2, rows, basis)
+
+
 def solution(mesh):
-    placed = (P("ka", None, "ba", None), P("ka", "ba", None), P(), P())
-    return jax.shard_map(
-        per_device, mesh=mesh, in_specs=placed, out_specs=P("ka", None, "ba", None), check_vma=False
-    )
+    sizes = mesh.shape
+    width, lines = sizes["ka"], sizes["ba"]
+    columns = (P("ka", None, "ba", None), P("ka", "ba", None), P(), P())
+
+    def run(green_irr, screened, kmap, rotation):
+        rows = green_irr.shape[2] // lines
+        near = screened.shape[0] // width
+        parts = width // HALVES
+        if green_irr.shape[0] != width or width % HALVES or rows % (parts * ORB * 8) or near % 16:
+            return jax.shard_map(
+                per_device_columns,
+                mesh=mesh,
+                in_specs=columns,
+                out_specs=P("ka", None, "ba", None),
+                check_vma=False,
+            )(green_irr, screened, kmap, rotation)
+        finer = Mesh(mesh.devices.reshape(HALVES, parts, lines), ("kh", "kl", "ba"))
+        both = ("kh", "kl")
+        placed = (P(both, None, "ba", None), P(both, "ba", None), P(), P())
+        return jax.shard_map(
+            per_device_rows,
+            mesh=finer,
+            in_specs=placed,
+            out_specs=P(both, None, "ba", None),
+            check_vma=False,
+        )(green_irr, screened, kmap, rotation)
+
+    return run

time: 584 us -> 135 us (0.23)
  the two profiles are of different devices: /device:TPU:0 before, /device:TPU:26 now
where the time goes in v4:
time: 135 us
  Pallas kernels  127 us (94%)
  other arithmetic  3.25 us (2%)
  local copies, waits for them, and re-layouts  2.45 us (2%)
  matrix products  1.78 us (1%)
    pallas_call x1, Pallas kernels, per_device_rows(): pl.pallas_call(functools.partial(kernel, halves, width), in_specs=[vmem]...  127 us

profile of v4, /device:TPU:26, one launch (start us, length us, event | category | flops | bytes accessed | tf_op | source)
XLA Modules:
  0.0 134.6 jit_solution(12556661012291851537)
XLA Ops:
  0.0 0.0 copy-start.2
  0.0 0.7 multiply_bitcast_fusion
  0.8 0.4 fusion.17
  1.1 0.4 cosine_convert_fusion
  1.5 0.1 dynamic-slice_maximum_fusion.back_ref
  1.6 0.0 copy-start
  1.6 0.0 copy-start.1
  1.6 0.1 fusion.8.swap_ref
  1.7 1.8 %fusion.3.code_ref = bf16[128,768]{1,0:T(8,128)(2,1)S(1)} fusion(s32[768]{0:T(1024)S(1)} %get-tuple-element.7, s32[128,768]{1,0:T(8,128)} %param.7, s32[768]{0:T(1024)S(1)} %get-tuple-element.8), kind=kOutput, calls=%fused_computation.4 | convolution fusion | flops 152469504 | bytes 595968 | tf_op jit(solution)/shard_map/dot_general | solution.py:413
  3.5 0.1 fusion.4.site_ref
  3.6 0.0 copy-done.2
  3.7 0.1 fusion.6
  3.7 0.1 fusion.13
  3.9 0.1 copy.6
  4.0 1.3 fusion.1.order_ref
  5.2 0.0 copy-done
  5.2 0.0 copy-done.1
  5.2 127.0 %shard_map.46 = f32[2,192,768]{2,1,0:T(8,128)} custom-call(bf16[256,256]{1,0:T(8,128)(2,1)S(1)} %fusion.8.swap_ref, bf16[768,768]{1,0:T(8,128)(2,1)} %fusion.1.order_ref, bf16[384,384]{1,0:T(8,128)(2,1)S(1)} %fusion.4.site_ref, bf16[384,768]{1,0:T(8,128)(2,1)S(1)} %bitcast.7, bf16[16,192,768]{2,1,0:T(8,128)(2,1)} %w_ref.1, ...), custom_call_target="tpu_custom_call" | custom-call | flops 60000002048 | bytes 12582912 | tf_op jit(solution)/shard_map/pallas_call | solution.py:424
  132.3 2.4 %copy.8 = f32[1,2,192,768]{3,2,1,0:T(8,128)} copy(f32[1,2,192,768]{3,2,1,0:T(8,128)} %bitcast.9) | data formatting | bytes 2359296
  (7 shorter events, 0.1 us)
Async XLA Ops:
  0.0 3.6 %copy-start.2 = (s32[128,768]{1,0:T(8,128)S(1)}, s32[128,768]{1,0:T(8,128)}, u32[]{:S(2)}) copy-start(s32[128,768]{1,0:T(8,128)} %param.7) | copy-start | bytes 1179652
  1.6 3.6 %copy-start = (bf16[1,2,192,768]{3,2,1,0:T(8,128)(2,1)S(1)}, bf16[1,2,192,768]{3,2,1,0:T(8,128)(2,1)}, u32[]{:S(2)}) copy-start(bf16[1,2,192,768]{3,2,1,0:T(8,128)(2,1)} %param.4) | copy-start | bytes 1769476
  1.6 3.6 %copy-start.1 = (s32[128,1]{0,1:T(1,128)S(1)}, s32[128,1]{0,1:T(1,128)}, u32[]{:S(2)}) copy-start(s32[128,1]{0,1:T(1,128)} %param.6) | copy-start | bytes 1540

commit v5 on v4

--- a/solution.py
+++ b/solution.py
@@ -290,11 +290,9 @@
 
     lax.fori_loop(0, sites, unfold, 0)
 
-    def w_arrived(t, carry):
-        w_copy(t).wait_recv()
-        return carry
-
-    lax.fori_loop(0, blocks * (width - 1), w_arrived, 0)
+    def w_arrived(b):
+        for t in range(b * (width - 1), (b + 1) * (width - 1)):
+            w_copy(t).wait_recv()
 
     point = lax.broadcasted_iota(jnp.int32, (count, zone), 0) // ORB
     named = jnp.where(point == target_ref[...], 1.0, 0.0)
@@ -311,40 +309,56 @@
             device_id_type=pl.DeviceIdType.MESH,
         )
 
+    def fold(c, site):
+        for oa in range(ORB):
+            row = site * ORB + oa
+            if c == 0:
+                w = w_recv[:, row].reshape(here, basis).astype(f32)
+                sigma = (-(green_r[row].astype(f32) * w)).astype(bf16)
+                green_r[row] = sigma
+            else:
+                sigma = green_r[row]
+            full[oa, 0:zone] = jnp.dot(
+                back_ref[c * zone : (c + 1) * zone, :], sigma, preferred_element_type=f32
+            ).astype(bf16)
+
+        def read(oa, c, p, at):
+            at = pl.ds(pl.multiple_of(at * 16, 16), 16)
+            return full[oa, at, p * atoms : (p + 1) * atoms]
+
+        def write(oa, c, o, at, value):
+            at = pl.ds(pl.multiple_of(oa * zone + at * 16, 16), 16)
+            half[at, o * atoms : (o + 1) * atoms] = value
+
+        turn_columns(coef_ref, (c,), read, write, zone, True)
+        sums = jnp.dot(
+            site_select(rows_ref, site, count), half[:, 0:basis], preferred_element_type=f32
+        )
+        stage[c, site] = (sums / counts).astype(bf16)
+
+    starts = [b * step // ORB for b in range(blocks)]
+
+    def fold_both(site, carry):
+        for b in range(blocks - 1):
+            pl.when(site == starts[b])(functools.partial(w_arrived, b))
+        fold(0, site)
+        fold(1, site)
+        return carry
+
+    lax.fori_loop(0, starts[-1], fold_both, 0)
+    w_arrived(blocks - 1)
     for c in range(2):
 
-        def fold(site, carry, c=c):
-            for oa in range(ORB):
-                row = site * ORB + oa
-                if c == 0:
-                    w = w_recv[:, row].reshape(here, basis).astype(f32)
-                    sigma = (-(green_r[row].astype(f32) * w)).astype(bf16)
-                    green_r[row] = sigma
-                else:
-                    sigma = green_r[row]
-                full[oa, 0:zone] = jnp.dot(
-                    back_ref[c * zone : (c + 1) * zone, :], sigma, preferred_element_type=f32
-                ).astype(bf16)
-
-            def read(oa, c, p, at):
-                at = pl.ds(pl.multiple_of(at * 16, 16), 16)
-                return full[oa, at, p * atoms : (p + 1) * atoms]
-
-            def write(oa, c, o, at, value):
-                at = pl.ds(pl.multiple_of(oa * zone + at * 16, 16), 16)
-                half[at, o * atoms : (o + 1) * atoms] = value
-
-            turn_columns(coef_ref, (c,), read, write, zone, True)
-            sums = jnp.dot(
-                site_select(rows_ref, site, count), half[:, 0:basis], preferred_element_type=f32
-            )
-            stage[site] = (sums / counts).astype(bf16)
+        def fold_one(site, carry, c=c):
+            fold(c, site)
             return carry
 
-        lax.fori_loop(0, sites, fold, 0)
+        lax.fori_loop(starts[-1], sites, fold_one, 0)
         o_send[:, c] = (
             jnp.dot(
-                site_ref[...], stage[...].reshape(sites * count, basis), preferred_element_type=f32
+                site_ref[...],
+                stage[c].reshape(sites * count, basis),
+                preferred_element_type=f32,
             )
             .astype(bf16)
             .reshape(total, part, basis)
@@ -436,7 +450,7 @@
             pltpu.VMEM((ORB, ORB, zone, basis // ORB), bf16),
             pltpu.VMEM((ORB * zone, 2 * basis), bf16),
             pltpu.VMEM((ORB, 2 * zone, basis), bf16),
-            pltpu.VMEM((sites, count, basis), bf16),
+            pltpu.VMEM((2, sites, count, basis), bf16),
             pltpu.VMEM((total, 2, part, basis), bf16),
             pltpu.VMEM((total, 2, part, basis), bf16),
             pltpu.SemaphoreType.DMA((total - 1,)),

time: 135 us -> 123 us (0.911)
  the two profiles are of different devices: /device:TPU:26 before, /device:TPU:30 now
where the time goes in v5:
time: 123 us
  Pallas kernels  116 us (94%)
  other arithmetic  3.25 us (3%)
  local copies, waits for them, and re-layouts  2.45 us (2%)
  matrix products  1.78 us (1%)
    pallas_call x1, Pallas kernels, per_device_rows(): pl.pallas_call(functools.partial(kernel, halves, width), in_specs=[vmem]...  116 us

profile of v5, /device:TPU:30, one launch (start us, length us, event | category | flops | bytes accessed | tf_op | source)
XLA Modules:
  0.0 123.3 jit_solution(8329202973454722310)
XLA Ops:
  0.0 0.0 copy-start.2
  0.0 0.7 multiply_bitcast_fusion
  0.8 0.4 fusion.17
  1.1 0.4 cosine_convert_fusion
  1.5 0.1 dynamic-slice_maximum_fusion.back_ref
  1.6 0.0 copy-start
  1.6 0.0 copy-start.1
  1.6 0.1 fusion.8.swap_ref
  1.7 1.8 %fusion.3.code_ref = bf16[128,768]{1,0:T(8,128)(2,1)S(1)} fusion(s32[768]{0:T(1024)S(1)} %get-tuple-element.7, s32[128,768]{1,0:T(8,128)} %param.7, s32[768]{0:T(1024)S(1)} %get-tuple-element.8), kind=kOutput, calls=%fused_computation.4 | convolution fusion | flops 152469504 | bytes 595968 | tf_op jit(solution)/shard_map/dot_general | solution.py:427
  3.5 0.1 fusion.4.site_ref
  3.6 0.0 copy-done.2
  3.7 0.1 fusion.6
  3.7 0.1 fusion.13
  3.9 0.1 copy.6
  4.0 1.3 %fusion.1.order_ref = bf16[768,768]{1,0:T(8,128)(2,1)} fusion(s32[768]{0:T(1024)S(1)} %get-tuple-element.7), kind=kLoop, calls=%fused_computation.2 | loop fusion | flops 1179648 | bytes 1182720 | tf_op jit(solution)/shard_map/convert_element_type | solution.py:124
  5.2 0.0 copy-done
  5.2 0.0 copy-done.1
  5.2 115.7 %shard_map.46 = f32[2,192,768]{2,1,0:T(8,128)} custom-call(bf16[256,256]{1,0:T(8,128)(2,1)S(1)} %fusion.8.swap_ref, bf16[768,768]{1,0:T(8,128)(2,1)} %fusion.1.order_ref, bf16[384,384]{1,0:T(8,128)(2,1)S(1)} %fusion.4.site_ref, bf16[384,768]{1,0:T(8,128)(2,1)S(1)} %bitcast.7, bf16[16,192,768]{2,1,0:T(8,128)(2,1)} %w_ref.1, ...), custom_call_target="tpu_custom_call" | custom-call | flops 60000002048 | bytes 12582912 | tf_op jit(solution)/shard_map/pallas_call | solution.py:438
  120.9 2.4 %copy.8 = f32[1,2,192,768]{3,2,1,0:T(8,128)} copy(f32[1,2,192,768]{3,2,1,0:T(8,128)} %bitcast.9) | data formatting | bytes 2359296
  (7 shorter events, 0.1 us)
Async XLA Ops:
  0.0 3.6 %copy-start.2 = (s32[128,768]{1,0:T(8,128)S(1)}, s32[128,768]{1,0:T(8,128)}, u32[]{:S(2)}) copy-start(s32[128,768]{1,0:T(8,128)} %param.7) | copy-start | bytes 1179652
  1.6 3.6 %copy-start = (bf16[1,2,192,768]{3,2,1,0:T(8,128)(2,1)S(1)}, bf16[1,2,192,768]{3,2,1,0:T(8,128)(2,1)}, u32[]{:S(2)}) copy-start(bf16[1,2,192,768]{3,2,1,0:T(8,128)(2,1)} %param.4) | copy-start | bytes 1769476
  1.6 3.6 %copy-start.1 = (s32[128,1]{0,1:T(1,128)S(1)}, s32[128,1]{0,1:T(1,128)}, u32[]{:S(2)}) copy-start(s32[128,1]{0,1:T(1,128)} %param.6) | copy-start | bytes 1540
